TPU v7x, 256 devices: a whole 4x4x8 slice. The times are simulated.
256 devices in a mesh: batch: 64 (over x, z, core), mp: 4 (over y).
Axes of the slice: x: 4, y: 4, z: 8, core: 2. Of those that a mesh axis runs over, the one named last changes fastest.
Arguments:
- query_hidden: bfloat16 [16384, 4096], P('batch', 'mp'), may hold values from -6 to 6
- positive_hidden: bfloat16 [16384, 4096], P('batch', 'mp'), may hold values from -6 to 6
- pool_hidden: bfloat16 [32768, 4096], P('batch', 'mp'), may hold values from -6 to 6
- norm_gain: float32 [4096], P('mp'), may hold values from 0.1 to 1.9
- hard_ids: int32 [16384, 3], P('batch'), may hold values from 0 to 32767, as said below
- location: int32 [32768], replicated, may hold values from 0 to 32767, as said below
- partner_masks: int32 [2], replicated, may hold values from 1 to 63
Outputs:
- query_loss: float32 [16384], P(('batch', 'mp'))
- grad_query: bfloat16 [16384, 4096], P('batch', 'mp')
- grad_positive: bfloat16 [16384, 4096], P('batch', 'mp')
- grad_pool: bfloat16 [32768, 4096], P('batch', 'mp')
Inputs may be any that keep to these rules, and one draw needn't show every extreme that they name: `hard_ids`: every entry is a passage id. With owner(p) = location[p] // 512: the 768 ids of the queries of one batch device are all different, at most 24 of them have one owner, and some owner is named exactly 24 times by the queries of every batch device. A permutation: passage id p is stored at row location[p] of the pool.
All inputs are finite; a program needn't handle non-finite values.
Results may differ from a plain program's by a relative error of at most 0.0073.
Values may be sent and summed in bfloat16 or wider, within the bound.
No kernel may reach another device: no remote copies, remote signals or barrier semaphores. Data moves between devices by JAX's collectives and lax.ppermute only.
A program may use at most 64 MiB of HBM per device.

v0:
```python
import jax
import jax.numpy as jnp
from jax import lax
from jax.experimental import pallas as pl
from jax.experimental.pallas import tpu as pltpu
from jax.sharding import PartitionSpec as P

MODEL_WIDTH = 4096
SOFTMAX_TEMPER = 0.02
EPSILON = 1e-06
FIXED = 32000.0
SCALE = MODEL_WIDTH / 64.0 / SOFTMAX_TEMPER
BF = jnp.bfloat16
F32 = jnp.float32


def exchanged(x):
    return lax.all_to_all(x, "batch", split_axis=0, concat_axis=0, tiled=True)


def scaled_rows(hidden, norm_gain):
    return norm_gain[None, :] * hidden.astype(F32)


def row_squares(hidden, norm_gain):
    scaled = scaled_rows(hidden, norm_gain)
    return jnp.sum(scaled * scaled, axis=1)


def embedding(hidden, norm_gain, inverse):
    return (scaled_rows(hidden, norm_gain) * inverse[:, None]).astype(BF)


def gradient(hidden, inverse, delta, product, norm_gain):
    inner = delta - scaled_rows(hidden, norm_gain) * (inverse * inverse * product)[:, None]
    return (norm_gain[None, :] * inverse[:, None] * inner).astype(BF)


def dot(a, b, dims=((1,), (0,))):
    return lax.dot_general(a, b, (dims, ((), ())), preferred_element_type=F32)


def one_hot(column, width):
    return (column[:, None] == jnp.arange(width, dtype=jnp.int32)[None, :]).astype(BF)


def looked_up(table, ids):
    rows = table.shape[0] // 128
    bytes_of = table.reshape(rows, 128)
    parts = jnp.concatenate([bytes_of >> 8, bytes_of & 255], axis=1).astype(BF)
    found = dot(one_hot(ids >> 7, rows), parts)
    value = found[:, :128] * 256.0 + found[:, 128:]
    lane = (ids & 127)[:, None] == jnp.arange(128, dtype=jnp.int32)[None, :]
    return jnp.sum(jnp.where(lane, value, 0.0), axis=1).astype(jnp.int32)


def after(x, value):
    return jnp.where(jnp.isnan(value.reshape(-1)[0].astype(F32)), jnp.zeros_like(x), x)


def summed(x):
    parts = lax.axis_size("mp")
    total = x
    for step in range(1, parts):
        total = total + lax.ppermute(x, "mp", [(i, (i + step) % parts) for i in range(parts)])
    return total


VMEM_BYTES = 40 * 1024 * 1024
GROUP = 8


def called(body, out_shape, flops, **more):
    return pl.pallas_call(
        body,
        out_shape=out_shape,
        compiler_params=pltpu.CompilerParams(vmem_limit_bytes=VMEM_BYTES),
        cost_estimate=pl.CostEstimate(flops=flops, bytes_accessed=8 << 20, transcendentals=0),
        **more,
    )


def lanes_of(shape):
    return lax.broadcasted_iota(jnp.int32, shape, 1)


def sublanes_of(shape):
    return lax.broadcasted_iota(jnp.int32, shape, 0)


def hot(matches):
    return matches.astype(F32).astype(BF)


def whole(shape):
    return pl.BlockSpec(shape, lambda i: (0,) * len(shape))


def split_value(value, lane, at):
    high = value.astype(BF).astype(F32)
    middle = (value - high).astype(BF).astype(F32)
    low = value - high - middle
    return jnp.where(
        lane == at, high, jnp.where(lane == at + 1, middle, jnp.where(lane == at + 2, low, 0.0))
    )


def served_rows(first, emb_pool, masks, steps, chunk):
    rows, width = first.shape
    pool, features = emb_pool.shape
    lines = rows // chunk * GROUP
    halves = GROUP // chunk

    def body(masks_ref, first_ref, pool_ref, out_ref, digits_ref):
        step = pl.program_id(0)
        line = sublanes_of((lines, 1))
        receiver = line // GROUP
        part = (line % GROUP) // chunk
        piece = line % chunk

        @pl.when(step == 0)
        def _():
            spreading = hot(lanes_of((lines, rows)) == receiver * chunk + piece)
            digits_ref[...] = dot(spreading, first_ref[:, features:])

        @pl.when(step < steps)
        def _():
            digits = digits_ref[...]
            lane = lanes_of(digits.shape)
            place = step * halves + part
            value = jnp.where(lane == place, digits * 16.0, 0.0)
            value = jnp.where(lane == place + 64, digits, value)
            asked = jnp.sum(value, axis=1, keepdims=True).astype(jnp.int32) - 1
            out_ref[...] = dot(hot(lanes_of((lines, pool)) == asked), pool_ref[...]).astype(BF)

        @pl.when(step == steps)
        def _():
            mask = jnp.where(part == 0, masks_ref[0], masks_ref[1])
            source = (receiver ^ mask) * chunk + piece
            chosen = hot(lanes_of((lines, rows)) == source)
            out_ref[...] = dot(chosen, first_ref[:, :features]).astype(BF)

    return called(
        body,
        pltpu.HBM((lines, (steps + 1) * features), BF),
        2 * lines * steps * pool * features,
        grid=(steps + 1,),
        in_specs=[
            pl.BlockSpec(memory_space=pltpu.SMEM),
            whole((rows, width)),
            whole((pool, features)),
        ],
        out_specs=pl.BlockSpec((lines, features), lambda i: (0, i)),
        scratch_shapes=[pltpu.VMEM((lines, 128), F32)],
    )(masks, first, emb_pool)


def partial_scores(turned_q, arrived, code, steps, parts):
    rows, features = turned_q.shape
    lines = arrived.shape[0]
    hard = code.shape[0]
    share = rows // parts

    def body(q_ref, arrived_ref, code_ref, emb_ref, kept_ref, *rest):
        *coded_refs, total_ref = rest
        step = pl.program_id(0)

        def score(candidates, at):
            count = candidates.shape[0]
            partial = dot(q_ref[...], candidates, ((1,), (1,)))
            kept_ref[:, at : at + count] = partial[:share]
            for i, ref in enumerate(coded_refs):
                coded = jnp.round(partial[(i + 1) * share : (i + 2) * share] * FIXED)
                ref[:, at : at + count] = coded.astype(jnp.int32).astype(jnp.int16)

        @pl.when(step == 0)
        def _():
            score(arrived_ref[...], 0)
            total_ref[...] = jnp.zeros_like(total_ref)

        @pl.when(step > 0)
        def _():
            chosen = hot(lanes_of((hard, lines)) + (step - 1) * lines == code_ref[...])
            total_ref[...] += dot(chosen, arrived_ref[...])

        @pl.when(step == steps)
        def _():
            emb_ref[...] = total_ref[...].astype(BF)
            score(emb_ref[...], lines)

    columns = lines + hard
    return called(
        body,
        [jax.ShapeDtypeStruct((hard, features), BF), jax.ShapeDtypeStruct((share, columns), F32)]
        + [jax.ShapeDtypeStruct((share, columns), jnp.int16)] * (parts - 1),
        2 * hard * steps * lines * features,
        grid=(steps + 1,),
        in_specs=[
            whole((rows, features)),
            pl.BlockSpec((lines, features), lambda i: (0, (i + steps) % (steps + 1))),
            whole((hard, 1)),
        ],
        out_specs=[whole((hard, features))] + [whole((share, columns))] * parts,
        scratch_shapes=[pltpu.VMEM((hard, features), F32)],
    )(turned_q, arrived, code[:, None])


def outgoing_rows(pieces, code, values, turned_q, lines, steps):
    share, columns = pieces[0].shape
    rows, features = turned_q.shape
    hard = code.shape[0]
    tile = lines // 2

    def body(*refs):
        code_ref, near_ref, far_ref, q_ref, out_ref, all_ref = refs[len(pieces) :]
        step = pl.program_id(0)

        @pl.when(step == 0)
        def _():
            for i, ref in enumerate(refs[: len(pieces)]):
                all_ref[i * share : (i + 1) * share, :] = ref[...]

        lane = lanes_of((tile, 128))
        line = sublanes_of((tile, hard)) + step * tile
        extra = jnp.zeros((tile, 128), F32)
        for t in range(steps):
            matches = line + t * lines == code_ref[...]
            value = jnp.sum(jnp.where(matches, far_ref[...], 0.0), axis=1, keepdims=True)
            extra = extra + split_value(value, lane, 3 * t)
            weights = dot(hot(matches), all_ref[:, lines:], ((1,), (1,))).astype(BF)
            out_ref[:, t * features : (t + 1) * features] = dot(weights, q_ref[...]).astype(BF)
        near = sublanes_of((tile, lines)) + step * tile == lanes_of((tile, lines))
        value = jnp.sum(jnp.where(near, near_ref[...], 0.0), axis=1, keepdims=True)
        extra = extra + split_value(value, lane, 3 * steps)
        weights = all_ref[:, pl.ds(pl.multiple_of(step * tile, tile), tile)]
        delta = dot(weights, q_ref[...], ((0,), (0,)))
        out_ref[:, steps * features : (steps + 1) * features] = delta.astype(BF)
        out_ref[:, (steps + 1) * features :] = extra.astype(BF)

    width = (steps + 1) * features + 128
    return called(
        body,
        pltpu.HBM((lines, width), BF),
        2 * lines * (steps + 1) * rows * (hard + features),
        grid=(2,),
        in_specs=[whole((share, columns))] * len(pieces)
        + [whole((1, hard)), whole((1, lines)), whole((1, hard)), whole((rows, features))],
        out_specs=pl.BlockSpec((tile, width), lambda i: (i, 0)),
        scratch_shapes=[pltpu.VMEM((rows, columns), BF)],
    )(
        *pieces,
        code[None, :],
        values[None, :lines],
        values[None, lines:],
        turned_q,
    )


def merged_rows(third, masks, rows, features, steps, chunk):
    lines, width = third.shape

    def body(masks_ref, near_ref, extra_ref, out_ref):
        line = lanes_of((1, lines))
        mask = jnp.where((line % GROUP) // chunk == 0, masks_ref[0], masks_ref[1])
        target = ((line // GROUP) ^ mask) * chunk + line % chunk
        back = hot(sublanes_of((rows, lines)) == target)
        out_ref[:, :features] = dot(back, near_ref[...]).astype(BF)
        lane = lanes_of((rows, 128))
        terms = dot(back, extra_ref[...])
        mine = (lane >= 3 * steps) & (lane < 3 * steps + 3)
        value = jnp.sum(jnp.where(mine, terms, 0.0), axis=1, keepdims=True)
        out_ref[:, features:] = split_value(value, lane, 0).astype(BF)

    return called(
        body,
        jax.ShapeDtypeStruct((rows, features + 128), BF),
        2 * rows * lines * features,
        grid=(1,),
        in_specs=[
            pl.BlockSpec(memory_space=pltpu.SMEM),
            pl.BlockSpec((lines, features), lambda i: (0, steps)),
            pl.BlockSpec((lines, 128), lambda i: (0, (steps + 1) * features // 128)),
        ],
        out_specs=whole((rows, features + 128)),
    )(masks, third, third)


def pool_gradient(third, asked, pool_hidden, inverse, norm_gain):
    lines, width = third.shape
    pool, features = pool_hidden.shape
    steps = asked.shape[0]
    tile = 256

    def body(third_ref, asked_ref, hidden_ref, inverse_ref, gain_ref, out_ref):
        row = sublanes_of((tile, lines)) + pl.program_id(0) * tile
        delta = jnp.zeros((tile, features), F32)
        value = jnp.zeros((tile, 1), F32)
        lane = lanes_of((tile, 128))
        for t in range(steps):
            back = hot(row == asked_ref[t : t + 1, :])
            delta = delta + dot(back, third_ref[:, t * features : (t + 1) * features])
            terms = dot(back, third_ref[:, width - 128 :])
            mine = (lane >= 3 * t) & (lane < 3 * t + 3)
            value = value + jnp.sum(jnp.where(mine, terms, 0.0), axis=1, keepdims=True)
        gain = gain_ref[...]
        scaled = gain * hidden_ref[...].astype(F32)
        inner = delta - scaled * (inverse_ref[...] * value)
        out_ref[...] = (gain * inverse_ref[...] * inner).astype(BF)

    tiled = lambda n: pl.BlockSpec((tile, n), lambda i: (i, 0))
    return called(
        body,
        jax.ShapeDtypeStruct((pool, features), BF),
        2 * pool * lines * steps * features,
        grid=(pool // tile,),
        in_specs=[
            whole((lines, width)),
            whole((steps, lines)),
            tiled(features),
            tiled(1),
            whole((1, features)),
        ],
        out_specs=tiled(features),
    )(third, asked, pool_hidden, inverse[:, None], norm_gain[None, :])


def per_device(
    query_hidden, positive_hidden, pool_hidden, norm_gain, hard_ids, location, partner_masks
):
    devices = lax.axis_size("batch")
    parts = lax.axis_size("mp")
    me_mp = lax.axis_index("mp")
    rows_dev, feature_dev = query_hidden.shape
    pool_dev = pool_hidden.shape[0]
    hard_count = hard_ids.shape[0] * hard_ids.shape[1]
    capacity = max(hard_count // 32, 2 * ((hard_count + devices - 1) // devices))
    steps = (capacity + GROUP - 1) // GROUP
    chunk = rows_dev // devices
    lines = devices * GROUP
    share = rows_dev // parts
    int_range = lambda n: jnp.arange(n, dtype=jnp.int32)

    partial_squares = jnp.concatenate(
        [row_squares(x, norm_gain) for x in (positive_hidden, query_hidden, pool_hidden)]
    )
    inverse = lax.rsqrt(summed(partial_squares) + EPSILON)
    inverse_p, inverse_q, inverse_pool = jnp.split(inverse, [rows_dev, 2 * rows_dev])
    emb_p = embedding(positive_hidden, norm_gain, inverse_p)

    ids = after(hard_ids, partial_squares).T.reshape(-1)
    storage = looked_up(location, ids)
    owners = storage // pool_dev
    local_row = storage % pool_dev
    order = int_range(hard_count)
    earlier = (owners[:, None] == owners[None, :]) & (order[None, :] < order[:, None])
    slot_index = jnp.sum(earlier.astype(jnp.int32), axis=1)
    line = slot_index % GROUP
    group = slot_index // GROUP
    code = group * lines + owners * GROUP + line
    lane = group * (GROUP // chunk) + line // chunk
    lanes = int_range(128)[None, :]
    wanted = local_row + 1
    digits = jnp.where(
        lanes == lane[:, None],
        (wanted >> 4)[:, None],
        jnp.where(lanes == lane[:, None] + 64, (wanted & 15)[:, None], 0),
    ).astype(BF)
    request_line = one_hot(owners * chunk + line % chunk, devices * chunk)
    requests = dot(request_line, digits, ((0,), (0,))).astype(BF)

    first = exchanged(
        jnp.concatenate(
            [
                emb_p.reshape(devices, chunk, feature_dev),
                requests.reshape(devices, chunk, 128),
            ],
            axis=2,
        )
    ).reshape(rows_dev, feature_dev + 128)
    halves = GROUP // chunk
    asked = first[:, feature_dev:].reshape(devices, chunk, 128).astype(jnp.int32)
    asked = asked[:, :, : steps * halves] * 16 + asked[:, :, 64 : 64 + steps * halves] - 1
    asked = asked.reshape(devices, chunk, steps, halves).transpose(2, 0, 3, 1).reshape(steps, lines)

    emb_q = embedding(query_hidden, norm_gain, inverse_q)
    emb_pool = embedding(pool_hidden, norm_gain, inverse_pool)
    turned_q = lax.dynamic_slice_in_dim(
        jnp.concatenate([emb_q, emb_q], axis=0), me_mp * share, rows_dev
    )

    arrived = exchanged(served_rows(first, emb_pool, partner_masks, steps, chunk))

    own_parts = dot(turned_q, emb_p, ((1,), (1,)))
    scores_own = own_parts[:share]
    for step in range(1, parts):
        scores_own = scores_own + lax.ppermute(
            own_parts[step * share : (step + 1) * share],
            "mp",
            [(i, (i + step) % parts) for i in range(parts)],
        )
    scores_own = scores_own / SOFTMAX_TEMPER
    hard_emb, kept, *coded = partial_scores(turned_q, arrived, code, steps, parts)
    total = jnp.zeros_like(kept)
    for step in range(1, parts):
        total = total + lax.ppermute(
            coded[step - 1], "mp", [(i, (i + step) % parts) for i in range(parts)]
        ).astype(F32)
    scores_far = (kept + total * (1.0 / FIXED)) * (1.0 / SOFTMAX_TEMPER)
    exp_own = jnp.exp(scores_own)
    exp_far = jnp.exp(scores_far)
    sums = jnp.sum(exp_own, axis=1) + jnp.sum(exp_far, axis=1)
    own = int_range(share)[:, None] + me_mp * share == int_range(rows_dev)[None, :]
    losses = jnp.log(sums) - jnp.sum(jnp.where(own, scores_own, 0.0), axis=1)
    ratio = 1.0 / sums
    weights_own = ((exp_own * ratio[:, None] - own.astype(F32)) * SCALE).astype(BF)
    weights_far = (exp_far * ratio[:, None] * SCALE).astype(BF)

    def gathered(piece):
        pieces = [piece]
        for step in range(1, parts):
            pieces.append(
                lax.ppermute(piece, "mp", [((i + step) % parts, i) for i in range(parts)])
            )
        return pieces

    values = summed(
        jnp.concatenate(
            [
                jnp.sum(weights_far.astype(F32) * scores_far, axis=0),
                jnp.sum(weights_own.astype(F32) * scores_own, axis=0),
            ]
        )
        * SOFTMAX_TEMPER
    )
    far_pieces = gathered(weights_far)
    columns = lines + hard_count
    third = exchanged(
        outgoing_rows(far_pieces, code, values[:columns], turned_q, lines, steps)
    )
    weights_own = jnp.concatenate(gathered(weights_own), axis=0)
    weights_far = jnp.concatenate(far_pieces, axis=0)

    def natural(x):
        return lax.dynamic_slice_in_dim(
            jnp.concatenate([x, x], axis=0), (parts - me_mp) * share, rows_dev
        )

    def row_products(hidden, delta):
        return summed(jnp.sum(scaled_rows(hidden, norm_gain) * delta, axis=1))

    delta_q = natural(
        dot(weights_own, emb_p)
        + dot(weights_far[:, :lines], arrived[:, steps * feature_dev :])
        + dot(weights_far[:, lines:], hard_emb)
    )
    product_q = summed(jnp.sum(scaled_rows(query_hidden, norm_gain) * delta_q, axis=1))
    grad_q = gradient(query_hidden, inverse_q, delta_q, product_q, norm_gain)
    delta_own = dot(weights_own, turned_q, ((0,), (0,)))

    masks = after(after(partner_masks, grad_q), delta_own)
    merged = merged_rows(third, masks, rows_dev, feature_dev, steps, chunk)
    home = exchanged(merged)
    grad_pool = pool_gradient(third, asked, pool_hidden, inverse_pool, norm_gain)
    home = home.astype(F32)
    delta_p = delta_own + home[:, :feature_dev]
    value_p = values[columns:] + jnp.sum(home[:, feature_dev : feature_dev + 3], axis=1)
    grad_p = gradient(positive_hidden, inverse_p, delta_p, value_p / inverse_p, norm_gain)
    return (losses, grad_q, grad_p, grad_pool)


def solution(mesh):
    placed = (
        P("batch", "mp"),
        P("batch", "mp"),
        P("batch", "mp"),
        P("mp"),
        P("batch", None),
        P(),
        P(),
    )
    return jax.shard_map(
        per_device,
        mesh=mesh,
        in_specs=placed,
        out_specs=(P(("batch", "mp")), P("batch", "mp"), P("batch", "mp"), P("batch", "mp")),
        check_vma=False,
    )
```

profile of v0, /device:TPU:1, one launch (start us, length us, event | category | flops | bytes accessed | tf_op | source)
XLA Modules:
  0.0 329.4 jit_solution(11484874430169157821)
XLA Ops:
  0.7 1.6 multiply_reduce_fusion
  2.3 1.6 multiply_reduce_fusion.3
  4.0 3.8 %collective-permute-start.1 = (f32[1024]{0:T(1024)S(1)}, f32[1024]{0:T(1024)S(1)}, u32[]{:S(2)}, u32[]{:S(2)}) collective-permute-start(f32[1024]{0:T(1024)S(1)} %pad_maximum_fusion.10), channel_id=1, source_target_pairs={{0,2},{1,3},{2,0},{3,1},{4,6},{5,7},{6,4},{7,5},{8,10},{9,11},{10,... | collective-permute-start | bytes 12296 | tf_op jit(solution)/shard_map/ppermute | solution.py:65
  7.8 0.8 collective-permute-start.2
  8.6 0.7 collective-permute-start
  12.1 0.9 convolution_convert_fusion
  13.1 1.0 multiply_convert_fusion.2
  14.3 1.1 pad_maximum_fusion
  15.4 13.3 %all-to-all-start = ((bf16[64,4,1152]{2,1,0:T(4,128)(2,1)}), bf16[64,4,1152]{2,1,0:T(4,128)(2,1)}, u32[]{:S(2)}, u32[]{:S(2)}) async-start(bf16[64,4,1152]{2,1,0:T(4,128)(2,1)} %pad_maximum_fusion), calls=%async_computation | async-start | bytes 1179648 | tf_op jit(solution)/shard_map/all_to_all | solution.py:18
  29.1 18.4 %all-to-all-done = bf16[64,4,1152]{2,1,0:T(4,128)(2,1)} async-done(((bf16[64,4,1152]{2,1,0:T(4,128)(2,1)}), bf16[64,4,1152]{2,1,0:T(4,128)(2,1)}, u32[]{:S(2)}, u32[]{:S(2)}) %all-to-all-start) | async-done | bytes 589856 | tf_op jit(solution)/shard_map/all_to_all | solution.py:18
  47.4 1.5 reshape.413.first_ref
  48.9 5.4 %shard_map.102 = bf16[512,4096]{1,0:T(8,128)(2,1)} custom-call(s32[2]{0:T(128)S(1)} %copy-done.2, bf16[256,1152]{1,0:T(8,128)(2,1)S(1)} %reshape.413.first_ref, bf16[512,1024]{1,0:T(8,128)(2,1)S(1)} %multiply_convert_fusion.pool_ref), custom_call_target="tpu_custom_call" | custom-call | flops 1610612736 | bytes 8388608 | tf_op jit(solution)/shard_map/pallas_call | solution.py:143
  54.3 6.6 %all-to-all-start.1 = ((bf16[64,8,4096]{2,1,0:T(8,128)(2,1)}), bf16[64,8,4096]{2,1,0:T(8,128)(2,1)}, u32[]{:S(2)}, u32[]{:S(2)}) async-start(bf16[64,8,4096]{2,1,0:T(8,128)(2,1)} %bitcast.37), calls=%async_computation.1 | async-start | bytes 8388608 | tf_op jit(solution)/shard_map/all_to_all | solution.py:18
  60.9 0.7 fusion.22.code_ref
  61.6 1.4 fusion.13.q_ref.refs_7_
  63.4 0.7 fusion.76
  64.4 2.3 collective-permute-start.5
  67.2 89.6 %all-to-all-done.1 = bf16[64,8,4096]{2,1,0:T(8,128)(2,1)} async-done(((bf16[64,8,4096]{2,1,0:T(8,128)(2,1)}), bf16[64,8,4096]{2,1,0:T(8,128)(2,1)}, u32[]{:S(2)}, u32[]{:S(2)}) %all-to-all-start.1) | async-done | bytes 4194336 | tf_op jit(solution)/shard_map/all_to_all | solution.py:18
  156.8 5.8 %shard_map.103 = (bf16[768,1024]{1,0:T(8,128)(2,1)S(1)}, f32[64,1280]{1,0:T(8,128)S(1)}, s16[64,1280]{1,0:T(8,128)(2,1)S(1)}, s16[64,1280]{1,0:T(8,128)(2,1)S(1)}, s16[64,1280]{1,0:T(8,128)(2,1)S(1)}) custom-call(bf16[256,1024]{1,0:T(8,128)(2,1)S(1)} %fusion.13.q_ref.refs_7_, bf16[512,4096]{1,0:T(8,128)(2,1)} %bitcast.7.arrived_ref, ...), custom_call_target="tpu_custom_call" | custom-call | flops 2415919104 | bytes 8388608 | tf_op jit(solution)/shard_map/pallas_call | solution.py:192
  163.1 2.8 collective-permute-start.7
  165.9 1.0 exponential_reduce_fusion.1
  166.8 2.5 collective-permute-done.6
  169.4 4.0 %collective-permute-done.7 = s16[64,1280]{1,0:T(8,128)(2,1)S(1)} collective-permute-done((s16[64,1280]{1,0:T(8,128)(2,1)S(1)}, s16[64,1280]{1,0:T(8,128)(2,1)S(1)}, u32[]{:S(2)}, u32[]{:S(2)}) %collective-permute-start.7) | collective-permute-done | bytes 163872 | tf_op jit(solution)/shard_map/ppermute | solution.py:405
  174.0 1.0 collective-permute-start.19
  175.0 2.5 collective-permute-start.20
  177.9 1.5 collective-permute-start.14
  179.4 2.0 collective-permute-start.13
  182.0 2.0 collective-permute-done.14.refs_3_
  184.0 3.5 %collective-permute-done.13.refs_2_ = bf16[64,1280]{1,0:T(8,128)(2,1)S(1)} collective-permute-done((bf16[64,1280]{1,0:T(8,128)(2,1)S(1)}, bf16[64,1280]{1,0:T(8,128)(2,1)S(1)}, u32[]{:S(2)}, u32[]{:S(2)}) %collective-permute-start.13) | collective-permute-done | bytes 163872 | tf_op jit(solution)/shard_map/ppermute | solution.py:422
  187.6 4.8 %shard_map.104 = bf16[512,4224]{1,0:T(8,128)(2,1)} custom-call(bf16[64,1280]{1,0:T(8,128)(2,1)S(1)} %get-tuple-element.25.refs_0_, bf16[64,1280]{1,0:T(8,128)(2,1)S(1)} %collective-permute-done.12.refs_1_, bf16[64,1280]{1,0:T(8,128)(2,1)S(1)} %collective-permute-done.13.refs_2_, bf16[64,1280]{1,0:T(8,128)(2,1)S(1)} %collective-permute-done.14.refs_3_, ...), custom_call_target="tpu_custom_call" | custom-call | flops 1879048192 | bytes 8388608 | tf_op jit(solution)/shard_map/pallas_call | solution.py:241
  192.3 8.2 %all-to-all-start.2 = ((bf16[64,8,4224]{2,1,0:T(8,128)(2,1)}), bf16[64,8,4224]{2,1,0:T(8,128)(2,1)}, u32[]{:S(2)}, u32[]{:S(2)}) async-start(bf16[64,8,4224]{2,1,0:T(8,128)(2,1)} %bitcast.36), calls=%async_computation.2 | async-start | bytes 8650752 | tf_op jit(solution)/shard_map/all_to_all | solution.py:18
  200.6 1.2 collective-permute-start.11
  201.8 2.3 collective-permute-start.10
  204.5 2.0 fusion.27
  206.5 1.7 fusion.6
  208.6 0.7 copy-done.7
  209.6 0.6 collective-permute-start.17
  210.2 2.3 collective-permute-start.16
  212.8 1.0 copy-done.4
  215.9 0.7 collective-permute-done.15
  218.9 80.3 %all-to-all-done.2 = bf16[64,8,4224]{2,1,0:T(8,128)(2,1)} async-done(((bf16[64,8,4224]{2,1,0:T(8,128)(2,1)}), bf16[64,8,4224]{2,1,0:T(8,128)(2,1)}, u32[]{:S(2)}, u32[]{:S(2)}) %all-to-all-start.2) | async-done | bytes 4325408 | tf_op jit(solution)/shard_map/all_to_all | solution.py:18
  299.3 1.8 shard_map.105
  301.1 1.0 all_to_all.30
  302.1 6.0 %all-to-all-start.3 = ((bf16[64,4,1152]{2,1,0:T(4,128)(2,1)}), bf16[64,4,1152]{2,1,0:T(4,128)(2,1)}, u32[]{:S(2)}, u32[]{:S(2)}) async-start(bf16[64,4,1152]{2,1,0:T(4,128)(2,1)} %all_to_all.30), calls=%async_computation.3 | async-start | bytes 1179648 | tf_op jit(solution)/shard_map/all_to_all | solution.py:18
  309.6 5.9 %shard_map.106 = bf16[512,1024]{1,0:T(8,128)(2,1)} custom-call(bf16[512,4224]{1,0:T(8,128)(2,1)} %bitcast.12.near_ref.extra_ref.third_ref, s32[3,512]{1,0:T(4,128)S(1)} %reshape.417.asked_ref, bf16[512,1024]{1,0:T(8,128)(2,1)S(1)} %copy-done, f32[512,1]{1,0:T(8,128)S(1)} %copy.34.inverse_ref, f32[1,1024]{1,0:T(1,128)S(1)} %bitcast.33), custom_call_target="tpu_custom_call" | custom-call | flops 1610612736 | bytes 8388608 | tf_op jit(solution)/shard_map/pallas_call | solution.py:311
  315.5 11.2 %all-to-all-done.3 = bf16[64,4,1152]{2,1,0:T(4,128)(2,1)} async-done(((bf16[64,4,1152]{2,1,0:T(4,128)(2,1)}), bf16[64,4,1152]{2,1,0:T(4,128)(2,1)}, u32[]{:S(2)}, u32[]{:S(2)}) %all-to-all-start.3) | async-done | bytes 589856 | tf_op jit(solution)/shard_map/all_to_all | solution.py:18
  326.7 1.4 reshape.418
  328.2 1.1 fusion.5
  (103 shorter events, 10.1 us)
Async XLA Ops:
  0.6 10.4 %copy-start.14 = (s32[256,3]{0,1:T(4,128)S(1)}, s32[256,3]{0,1:T(4,128)}, u32[]{:S(2)}) copy-start(s32[256,3]{0,1:T(4,128)} %param.11) | copy-start | bytes 9220
  0.6 10.5 %copy-start.13 = (s32[32768]{0:T(1024)S(1)}, s32[32768]{0:T(1024)}, u32[]{:S(2)}) copy-start(s32[32768]{0:T(1024)} %param.12) | copy-start | bytes 393220
  2.3 10.8 %copy-start.1 = (f32[1024]{0:T(1024)S(1)}, f32[1024]{0:T(1024)}, u32[]{:S(2)}) copy-start(f32[1024]{0:T(1024)} %param.10) | copy-start | bytes 12292
  2.3 10.8 %copy-start.6 = (bf16[256,1024]{1,0:T(8,128)(2,1)S(1)}, bf16[256,1024]{1,0:T(8,128)(2,1)}, u32[]{:S(2)}) copy-start(bf16[256,1024]{1,0:T(8,128)(2,1)} %param.7) | copy-start | bytes 1572868
  2.3 10.8 %copy-start.10 = (bf16[256,1024]{1,0:T(8,128)(2,1)S(1)}, bf16[256,1024]{1,0:T(8,128)(2,1)}, u32[]{:S(2)}) copy-start(bf16[256,1024]{1,0:T(8,128)(2,1)} %param.8) | copy-start | bytes 1572868
  4.0 9.1 %collective-permute-start.1 = (f32[1024]{0:T(1024)S(1)}, f32[1024]{0:T(1024)S(1)}, u32[]{:S(2)}, u32[]{:S(2)}) collective-permute-start(f32[1024]{0:T(1024)S(1)} %pad_maximum_fusion.10), channel_id=1, source_target_pairs={{0,2},{1,3},{2,0},{3,1},{4,6},{5,7},{6,4},{7,5},{8,10},{9,11},{10,... | collective-permute-start | bytes 12296 | tf_op jit(solution)/shard_map/ppermute | solution.py:65
  7.8 5.2 %collective-permute-start.2 = (f32[1024]{0:T(1024)S(1)}, f32[1024]{0:T(1024)S(1)}, u32[]{:S(2)}, u32[]{:S(2)}) collective-permute-start(f32[1024]{0:T(1024)S(1)} %pad_maximum_fusion.10), channel_id=1, source_target_pairs={{0,3},{1,0},{2,1},{3,2},{4,7},{5,4},{6,5},{7,6},{8,11},{9,8},{10,9... | collective-permute-start | bytes 12296 | tf_op jit(solution)/shard_map/ppermute | solution.py:65
  8.6 4.5 %collective-permute-start = (f32[1024]{0:T(1024)S(1)}, f32[1024]{0:T(1024)S(1)}, u32[]{:S(2)}, u32[]{:S(2)}) collective-permute-start(f32[1024]{0:T(1024)S(1)} %pad_maximum_fusion.10), channel_id=1, source_target_pairs={{0,1},{1,2},{2,3},{3,0},{4,5},{5,6},{6,7},{7,4},{8,9},{9,10},{10,1... | collective-permute-start | bytes 12296 | tf_op jit(solution)/shard_map/ppermute | solution.py:65
  14.1 14.9 %copy-start.8 = (bf16[256,1024]{1,0:T(8,128)(2,1)}, bf16[256,1024]{1,0:T(8,128)(2,1)S(1)}, u32[]{:S(2)}) copy-start(bf16[256,1024]{1,0:T(8,128)(2,1)S(1)} %get-tuple-element.41) | copy-start | bytes 1572868
  14.1 14.7 %copy-start = (bf16[512,1024]{1,0:T(8,128)(2,1)S(1)}, bf16[512,1024]{1,0:T(8,128)(2,1)}, u32[]{:S(2)}) copy-start(bf16[512,1024]{1,0:T(8,128)(2,1)} %hidden_ref.1) | copy-start | bytes 3145732
  15.4 33.5 %copy-start.2 = (s32[2]{0:T(128)S(1)}, s32[2]{0:T(128)}, u32[]{:S(2)}) copy-start(s32[2]{0:T(128)} %masks_ref.1) | copy-start | bytes 28
  15.4 32.0 %all-to-all-start = ((bf16[64,4,1152]{2,1,0:T(4,128)(2,1)}), bf16[64,4,1152]{2,1,0:T(4,128)(2,1)}, u32[]{:S(2)}, u32[]{:S(2)}) async-start(bf16[64,4,1152]{2,1,0:T(4,128)(2,1)} %pad_maximum_fusion), calls=%async_computation | async-start | bytes 1179648 | tf_op jit(solution)/shard_map/all_to_all | solution.py:18
  54.3 8.7 %copy-start.9 = (bf16[256,1024]{1,0:T(8,128)(2,1)S(1)}, bf16[256,1024]{1,0:T(8,128)(2,1)}, u32[]{:S(2)}) copy-start(bf16[256,1024]{1,0:T(8,128)(2,1)} %copy-done.8) | copy-start | bytes 1572868
  54.3 102.5 %all-to-all-start.1 = ((bf16[64,8,4096]{2,1,0:T(8,128)(2,1)}), bf16[64,8,4096]{2,1,0:T(8,128)(2,1)}, u32[]{:S(2)}, u32[]{:S(2)}) async-start(bf16[64,8,4096]{2,1,0:T(8,128)(2,1)} %bitcast.37), calls=%async_computation.1 | async-start | bytes 8388608 | tf_op jit(solution)/shard_map/all_to_all | solution.py:18
  64.1 101.8 %collective-permute-start.3 = (f32[64,256]{1,0:T(8,128)}, f32[64,256]{1,0:T(8,128)S(1)}, u32[]{:S(2)}, u32[]{:S(2)}) collective-permute-start(f32[64,256]{1,0:T(8,128)} %get-tuple-element.26), channel_id=1, source_target_pairs={{0,1},{1,2},{2,3},{3,0},{4,5},{5,6},{6,7},{7,4},{8,9},{9,10},{10,1... | collective-permute-start | bytes 196616 | tf_op jit(solution)/shard_map/ppermute | solution.py:396
  64.4 101.4 %collective-permute-start.5 = (f32[64,256]{1,0:T(8,128)}, f32[64,256]{1,0:T(8,128)S(1)}, u32[]{:S(2)}, u32[]{:S(2)}) collective-permute-start(f32[64,256]{1,0:T(8,128)} %get-tuple-element.27), channel_id=1, source_target_pairs={{0,3},{1,0},{2,1},{3,2},{4,7},{5,4},{6,5},{7,6},{8,11},{9,8},{10,9... | collective-permute-start | bytes 196616 | tf_op jit(solution)/shard_map/ppermute | solution.py:396
  66.7 99.1 %collective-permute-start.4 = (f32[64,256]{1,0:T(8,128)}, f32[64,256]{1,0:T(8,128)}, u32[]{:S(2)}, u32[]{:S(2)}) collective-permute-start(f32[64,256]{1,0:T(8,128)} %get-tuple-element.28), channel_id=1, source_target_pairs={{0,2},{1,3},{2,0},{3,1},{4,6},{5,7},{6,4},{7,5},{8,10},{9,11},{10,... | collective-permute-start | bytes 196616 | tf_op jit(solution)/shard_map/ppermute | solution.py:396
  162.6 29.7 %copy-start.3 = (bf16[768,1024]{1,0:T(8,128)(2,1)}, bf16[768,1024]{1,0:T(8,128)(2,1)S(1)}, u32[]{:S(2)}) copy-start(bf16[768,1024]{1,0:T(8,128)(2,1)S(1)} %get-tuple-element.13) | copy-start | bytes 4718596
  162.6 6.7 %collective-permute-start.6 = (s16[64,1280]{1,0:T(8,128)(2,1)S(1)}, s16[64,1280]{1,0:T(8,128)(2,1)S(1)}, u32[]{:S(2)}, u32[]{:S(2)}) collective-permute-start(s16[64,1280]{1,0:T(8,128)(2,1)S(1)} %get-tuple-element.10), channel_id=1, source_target_pairs={{0,1},{1,2},{2,3},{3,0},{4,5},{5,6},{6,7},{7,4},{8,9},{9,10},{10,1... | collective-permute-start | bytes 491528 | tf_op jit(solution)/shard_map/ppermute | solution.py:405
  163.1 10.3 %collective-permute-start.7 = (s16[64,1280]{1,0:T(8,128)(2,1)S(1)}, s16[64,1280]{1,0:T(8,128)(2,1)S(1)}, u32[]{:S(2)}, u32[]{:S(2)}) collective-permute-start(s16[64,1280]{1,0:T(8,128)(2,1)S(1)} %get-tuple-element.11), channel_id=1, source_target_pairs={{0,2},{1,3},{2,0},{3,1},{4,6},{5,7},{6,4},{7,5},{8,10},{9,11},{10,... | collective-permute-start | bytes 491528 | tf_op jit(solution)/shard_map/ppermute | solution.py:405
  165.8 7.5 %collective-permute-start.8 = (s16[64,1280]{1,0:T(8,128)(2,1)S(1)}, s16[64,1280]{1,0:T(8,128)(2,1)S(1)}, u32[]{:S(2)}, u32[]{:S(2)}) collective-permute-start(s16[64,1280]{1,0:T(8,128)(2,1)S(1)} %get-tuple-element.12), channel_id=1, source_target_pairs={{0,3},{1,0},{2,1},{3,2},{4,7},{5,4},{6,5},{7,6},{8,11},{9,8},{10,9... | collective-permute-start | bytes 491528 | tf_op jit(solution)/shard_map/ppermute | solution.py:405
  174.0 7.4 %collective-permute-start.19 = (f32[1536]{0:T(1024)S(1)}, f32[1536]{0:T(1024)S(1)}, u32[]{:S(2)}, u32[]{:S(2)}) collective-permute-start(f32[1536]{0:T(1024)S(1)} %maximum_multiply_fusion), channel_id=1, source_target_pairs={{0,2},{1,3},{2,0},{3,1},{4,6},{5,7},{6,4},{7,5},{8,10},{9,11},{10,... | collective-permute-start | bytes 18440 | tf_op jit(solution)/shard_map/ppermute | solution.py:65
  175.0 7.0 %collective-permute-start.20 = (f32[1536]{0:T(1024)S(1)}, f32[1536]{0:T(1024)S(1)}, u32[]{:S(2)}, u32[]{:S(2)}) collective-permute-start(f32[1536]{0:T(1024)S(1)} %maximum_multiply_fusion), channel_id=1, source_target_pairs={{0,3},{1,0},{2,1},{3,2},{4,7},{5,4},{6,5},{7,6},{8,11},{9,8},{10,9... | collective-permute-start | bytes 18440 | tf_op jit(solution)/shard_map/ppermute | solution.py:65
  177.4 4.5 %collective-permute-start.18 = (f32[1536]{0:T(1024)S(1)}, f32[1536]{0:T(1024)S(1)}, u32[]{:S(2)}, u32[]{:S(2)}) collective-permute-start(f32[1536]{0:T(1024)S(1)} %maximum_multiply_fusion), channel_id=1, source_target_pairs={{0,1},{1,2},{2,3},{3,0},{4,5},{5,6},{6,7},{7,4},{8,9},{9,10},{10,1... | collective-permute-start | bytes 18440 | tf_op jit(solution)/shard_map/ppermute | solution.py:65
  177.9 6.1 %collective-permute-start.14 = (bf16[64,1280]{1,0:T(8,128)(2,1)S(1)}, bf16[64,1280]{1,0:T(8,128)(2,1)S(1)}, u32[]{:S(2)}, u32[]{:S(2)}) collective-permute-start(bf16[64,1280]{1,0:T(8,128)(2,1)S(1)} %get-tuple-element.25.refs_0_), channel_id=1, source_target_pairs={{3,0},{0,1},{1,2},{2,3},{7,4},{4,5},{5,6},{6,7},{11,8},{8,9},{9,10... | collective-permute-start | bytes 491528 | tf_op jit(solution)/shard_map/ppermute | solution.py:422
  179.4 8.1 %collective-permute-start.13 = (bf16[64,1280]{1,0:T(8,128)(2,1)S(1)}, bf16[64,1280]{1,0:T(8,128)(2,1)S(1)}, u32[]{:S(2)}, u32[]{:S(2)}) collective-permute-start(bf16[64,1280]{1,0:T(8,128)(2,1)S(1)} %get-tuple-element.25.refs_0_), channel_id=1, source_target_pairs={{2,0},{3,1},{0,2},{1,3},{6,4},{7,5},{4,6},{5,7},{10,8},{11,9},{8,1... | collective-permute-start | bytes 491528 | tf_op jit(solution)/shard_map/ppermute | solution.py:422
  181.4 6.1 %collective-permute-start.12 = (bf16[64,1280]{1,0:T(8,128)(2,1)S(1)}, bf16[64,1280]{1,0:T(8,128)(2,1)S(1)}, u32[]{:S(2)}, u32[]{:S(2)}) collective-permute-start(bf16[64,1280]{1,0:T(8,128)(2,1)S(1)} %get-tuple-element.25.refs_0_), channel_id=1, source_target_pairs={{1,0},{2,1},{3,2},{0,3},{5,4},{6,5},{7,6},{4,7},{9,8},{10,9},{11,1... | collective-permute-start | bytes 491528 | tf_op jit(solution)/shard_map/ppermute | solution.py:422
  192.3 106.9 %all-to-all-start.2 = ((bf16[64,8,4224]{2,1,0:T(8,128)(2,1)}), bf16[64,8,4224]{2,1,0:T(8,128)(2,1)}, u32[]{:S(2)}, u32[]{:S(2)}) async-start(bf16[64,8,4224]{2,1,0:T(8,128)(2,1)} %bitcast.36), calls=%async_computation.2 | async-start | bytes 8650752 | tf_op jit(solution)/shard_map/all_to_all | solution.py:18
  200.6 7.7 %collective-permute-start.11 = (bf16[64,256]{1,0:T(8,128)(2,1)S(1)}, bf16[64,256]{1,0:T(8,128)(2,1)S(1)}, u32[]{:S(2)}, u32[]{:S(2)}) collective-permute-start(bf16[64,256]{1,0:T(8,128)(2,1)S(1)} %get-tuple-element.33), channel_id=1, source_target_pairs={{3,0},{0,1},{1,2},{2,3},{7,4},{4,5},{5,6},{6,7},{11,8},{8,9},{9,10... | collective-permute-start | bytes 98312 | tf_op jit(solution)/shard_map/ppermute | solution.py:422
  201.8 6.4 %collective-permute-start.10 = (bf16[64,256]{1,0:T(8,128)(2,1)S(1)}, bf16[64,256]{1,0:T(8,128)(2,1)S(1)}, u32[]{:S(2)}, u32[]{:S(2)}) collective-permute-start(bf16[64,256]{1,0:T(8,128)(2,1)S(1)} %get-tuple-element.33), channel_id=1, source_target_pairs={{2,0},{3,1},{0,2},{1,3},{6,4},{7,5},{4,6},{5,7},{10,8},{11,9},{8,1... | collective-permute-start | bytes 98312 | tf_op jit(solution)/shard_map/ppermute | solution.py:422
  204.1 4.1 %collective-permute-start.9 = (bf16[64,256]{1,0:T(8,128)(2,1)S(1)}, bf16[64,256]{1,0:T(8,128)(2,1)S(1)}, u32[]{:S(2)}, u32[]{:S(2)}) collective-permute-start(bf16[64,256]{1,0:T(8,128)(2,1)S(1)} %get-tuple-element.33), channel_id=1, source_target_pairs={{1,0},{2,1},{3,2},{0,3},{5,4},{6,5},{7,6},{4,7},{9,8},{10,9},{11,1... | collective-permute-start | bytes 98312 | tf_op jit(solution)/shard_map/ppermute | solution.py:422
  208.2 1.0 copy-start.7
  209.6 6.3 %collective-permute-start.17 = (f32[256]{0:T(256)S(1)}, f32[256]{0:T(256)S(1)}, u32[]{:S(2)}, u32[]{:S(2)}) collective-permute-start(f32[256]{0:T(256)S(1)} %multiply_reduce_fusion.1), channel_id=1, source_target_pairs={{0,3},{1,0},{2,1},{3,2},{4,7},{5,4},{6,5},{7,6},{8,11},{9,8},{10,9... | collective-permute-start | bytes 3080 | tf_op jit(solution)/shard_map/ppermute | solution.py:65
  210.2 5.7 %collective-permute-start.16 = (f32[256]{0:T(256)S(1)}, f32[256]{0:T(256)S(1)}, u32[]{:S(2)}, u32[]{:S(2)}) collective-permute-start(f32[256]{0:T(256)S(1)} %multiply_reduce_fusion.1), channel_id=1, source_target_pairs={{0,2},{1,3},{2,0},{3,1},{4,6},{5,7},{6,4},{7,5},{8,10},{9,11},{10,... | collective-permute-start | bytes 3080 | tf_op jit(solution)/shard_map/ppermute | solution.py:65
  212.5 4.0 %collective-permute-start.15 = (f32[256]{0:T(256)S(1)}, f32[256]{0:T(256)S(1)}, u32[]{:S(2)}, u32[]{:S(2)}) collective-permute-start(f32[256]{0:T(256)S(1)} %multiply_reduce_fusion.1), channel_id=1, source_target_pairs={{0,1},{1,2},{2,3},{3,0},{4,5},{5,6},{6,7},{7,4},{8,9},{9,10},{10,1... | collective-permute-start | bytes 3080 | tf_op jit(solution)/shard_map/ppermute | solution.py:65
  212.8 1.0 copy-start.4
  216.9 2.0 copy-start.12
  302.1 24.6 %all-to-all-start.3 = ((bf16[64,4,1152]{2,1,0:T(4,128)(2,1)}), bf16[64,4,1152]{2,1,0:T(4,128)(2,1)}, u32[]{:S(2)}, u32[]{:S(2)}) async-start(bf16[64,4,1152]{2,1,0:T(4,128)(2,1)} %all_to_all.30), calls=%async_computation.3 | async-start | bytes 1179648 | tf_op jit(solution)/shard_map/all_to_all | solution.py:18
  315.5 12.7 %copy-start.5 = (f32[256,1024]{1,0:T(8,128)S(1)}, f32[256,1024]{1,0:T(8,128)}, u32[]{:S(2)}) copy-start(f32[256,1024]{1,0:T(8,128)} %copy-done.4) | copy-start | bytes 3145732
  315.5 12.7 %copy-start.11 = (bf16[256,1024]{1,0:T(8,128)(2,1)S(1)}, bf16[256,1024]{1,0:T(8,128)(2,1)}, u32[]{:S(2)}) copy-start(bf16[256,1024]{1,0:T(8,128)(2,1)} %param.8) | copy-start | bytes 1572868
where the time goes:
time: 330 us; the launch traced here: 329 us
  waiting for transfers between devices  212 us (64%)
  starting transfers between devices  60.5 us (18%)
  Pallas kernels  23.8 us (7%)
  other arithmetic  12.5 us (4%)
  local copies, waits for them, and re-layouts  9.3 us (3%)
  matrix products  6 us (2%)
  between operations  5.13 us (2%)
    all_to_all x4, waiting for transfers between devices, exchanged(): return lax.all_to_all(x, 'batch', split_axis=0, concat_axis=0, tiled=True)  199 us
    all_to_all x4, starting transfers between devices, exchanged(): return lax.all_to_all(x, 'batch', split_axis=0, concat_axis=0, tiled=True)  34.1 us
    ppermute x9, starting transfers between devices, summed(): lax.ppermute(x, 'mp', [(i, (i + step) % parts) for i in range(parts)])  12.1 us
    ppermute x6, starting transfers between devices, gathered(): lax.ppermute(piece, 'mp', [((i + step) % parts, i) for i in range(parts)])  7.98 us
  transfers between devices with their start and end apart: 25, of which 9 were waited for; matrix products, arithmetic and copies ran while one was open for 4% of the time, Pallas kernels for 4%

commit v1 on v0

--- a/solution.py
+++ b/solution.py
@@ -161,7 +161,7 @@
     hard = code.shape[0]
     share = rows // parts
 
-    def body(q_ref, arrived_ref, code_ref, emb_ref, kept_ref, *rest):
+    def body(q_ref, arrived_ref, code_ref, kept_ref, *rest):
         *coded_refs, total_ref = rest
         step = pl.program_id(0)
 
@@ -185,13 +185,12 @@
 
         @pl.when(step == steps)
         def _():
-            emb_ref[...] = total_ref[...].astype(BF)
-            score(emb_ref[...], lines)
+            score(total_ref[...].astype(BF), lines)
 
     columns = lines + hard
     return called(
         body,
-        [jax.ShapeDtypeStruct((hard, features), BF), jax.ShapeDtypeStruct((share, columns), F32)]
+        [jax.ShapeDtypeStruct((share, columns), F32)]
         + [jax.ShapeDtypeStruct((share, columns), jnp.int16)] * (parts - 1),
         2 * hard * steps * lines * features,
         grid=(steps + 1,),
@@ -200,7 +199,7 @@
             pl.BlockSpec((lines, features), lambda i: (0, (i + steps) % (steps + 1))),
             whole((hard, 1)),
         ],
-        out_specs=[whole((hard, features))] + [whole((share, columns))] * parts,
+        out_specs=[whole((share, columns))] * parts,
         scratch_shapes=[pltpu.VMEM((hard, features), F32)],
     )(turned_q, arrived, code[:, None])
 
@@ -382,6 +381,7 @@
     asked = asked[:, :, : steps * halves] * 16 + asked[:, :, 64 : 64 + steps * halves] - 1
     asked = asked.reshape(devices, chunk, steps, halves).transpose(2, 0, 3, 1).reshape(steps, lines)
 
+    emb_p = embedding(positive_hidden, norm_gain, after(inverse_p, first))
     emb_q = embedding(query_hidden, norm_gain, inverse_q)
     emb_pool = embedding(pool_hidden, norm_gain, inverse_pool)
     turned_q = lax.dynamic_slice_in_dim(
@@ -399,7 +399,7 @@
             [(i, (i + step) % parts) for i in range(parts)],
         )
     scores_own = scores_own / SOFTMAX_TEMPER
-    hard_emb, kept, *coded = partial_scores(turned_q, arrived, code, steps, parts)
+    kept, *coded = partial_scores(turned_q, arrived, code, steps, parts)
     total = jnp.zeros_like(kept)
     for step in range(1, parts):
         total = total + lax.ppermute(
@@ -423,6 +423,7 @@
             )
         return pieces
 
+    far_pieces = gathered(weights_far)
     values = summed(
         jnp.concatenate(
             [
@@ -432,7 +433,6 @@
         )
         * SOFTMAX_TEMPER
     )
-    far_pieces = gathered(weights_far)
     columns = lines + hard_count
     third = exchanged(
         outgoing_rows(far_pieces, code, values[:columns], turned_q, lines, steps)
@@ -448,11 +448,15 @@
     def row_products(hidden, delta):
         return summed(jnp.sum(scaled_rows(hidden, norm_gain) * delta, axis=1))
 
-    delta_q = natural(
-        dot(weights_own, emb_p)
-        + dot(weights_far[:, :lines], arrived[:, steps * feature_dev :])
-        + dot(weights_far[:, lines:], hard_emb)
-    )
+    weights_slots = dot(weights_far[:, lines:], one_hot(code, steps * lines)).astype(BF)
+    weights_slots = jnp.concatenate([weights_slots, weights_far[:, :lines]], axis=1)
+    delta_q = dot(weights_own, emb_p)
+    for t in range(steps + 1):
+        delta_q = delta_q + dot(
+            weights_slots[:, t * lines : (t + 1) * lines],
+            arrived[:, t * feature_dev : (t + 1) * feature_dev],
+        )
+    delta_q = natural(delta_q)
     product_q = summed(jnp.sum(scaled_rows(query_hidden, norm_gain) * delta_q, axis=1))
     grad_q = gradient(query_hidden, inverse_q, delta_q, product_q, norm_gain)
     delta_own = dot(weights_own, turned_q, ((0,), (0,)))

time: 330 us -> 327 us (level)
  waiting for transfers between devices: 212 us -> 204 us
  matrix products: 6 us -> 11.4 us
    all_to_all x4, waiting for transfers between devices: 199 us -> 190 us  [exchanged(): return lax.all_to_all(x, 'batch', split_axis=0, concat_axis=0, tiled=True)]
    dot_general x7 -> x10, matrix products: 6 us -> 11.4 us  [dot(): return lax.dot_general(a, b, (dims, ((), ())), preferred_element_type=F32)]
  transfers between devices with their start and end apart: 25 -> 25, of which waited for: 9 -> 10; matrix products, arithmetic and copies ran while one was open for 4% -> 7% of each run, Pallas kernels for 4% -> 4%
where the time goes in v1:
time: 327 us; the launch traced here: 326 us
  waiting for transfers between devices  204 us (62%)
  starting transfers between devices  60.1 us (18%)
  Pallas kernels  23.6 us (7%)
  matrix products  11.4 us (3%)
  other arithmetic  11 us (3%)
  local copies, waits for them, and re-layouts  9.46 us (3%)
  between operations  6.46 us (2%)
    all_to_all x4, waiting for transfers between devices, exchanged(): return lax.all_to_all(x, 'batch', split_axis=0, concat_axis=0, tiled=True)  190 us
    all_to_all x4, starting transfers between devices, exchanged(): return lax.all_to_all(x, 'batch', split_axis=0, concat_axis=0, tiled=True)  34.2 us
    dot_general x10, matrix products, dot(): return lax.dot_general(a, b, (dims, ((), ())), preferred_element_type=F32)  11.4 us
    ppermute x6, starting transfers between devices, gathered(): lax.ppermute(piece, 'mp', [((i + step) % parts, i) for i in range(parts)])  10 us
    ppermute x9, starting transfers between devices, summed(): lax.ppermute(x, 'mp', [(i, (i + step) % parts) for i in range(parts)])  9.16 us
    ppermute x3, waiting for transfers between devices, per_device(): lax.ppermute(coded[step - 1], 'mp', [(i, (i + step) % parts) for i in ran...  8.73 us
  transfers between devices with their start and end apart: 25, of which 10 were waited for; matrix products, arithmetic and copies ran while one was open for 7% of the time, Pallas kernels for 4%

profile of v1, /device:TPU:1, one launch (start us, length us, event | category | flops | bytes accessed | tf_op | source)
XLA Modules:
  0.0 325.8 jit_solution(994229704131064922)
XLA Ops:
  0.7 1.6 multiply_reduce_fusion
  2.3 1.6 multiply_reduce_fusion.3
  3.9 3.6 %collective-permute-start.2 = (f32[1024]{0:T(1024)S(1)}, f32[1024]{0:T(1024)S(1)}, u32[]{:S(2)}, u32[]{:S(2)}) collective-permute-start(f32[1024]{0:T(1024)S(1)} %pad_maximum_fusion.5), channel_id=1, source_target_pairs={{0,3},{1,0},{2,1},{3,2},{4,7},{5,4},{6,5},{7,6},{8,11},{9,8},{10,9... | collective-permute-start | bytes 12296 | tf_op jit(solution)/shard_map/ppermute | solution.py:65
  7.9 0.7 collective-permute-start
  11.4 0.9 convolution_convert_fusion
  12.8 1.1 pad_maximum_fusion.1
  13.9 13.2 %all-to-all-start = ((bf16[64,4,1152]{2,1,0:T(4,128)(2,1)}), bf16[64,4,1152]{2,1,0:T(4,128)(2,1)S(1)}, u32[]{:S(2)}, u32[]{:S(2)}) async-start(bf16[64,4,1152]{2,1,0:T(4,128)(2,1)} %pad_maximum_fusion.1), calls=%async_computation | async-start | bytes 1179648 | tf_op jit(solution)/shard_map/all_to_all | solution.py:18
  27.4 18.4 %all-to-all-done = bf16[64,4,1152]{2,1,0:T(4,128)(2,1)S(1)} async-done(((bf16[64,4,1152]{2,1,0:T(4,128)(2,1)}), bf16[64,4,1152]{2,1,0:T(4,128)(2,1)S(1)}, u32[]{:S(2)}, u32[]{:S(2)}) %all-to-all-start) | async-done | bytes 589856 | tf_op jit(solution)/shard_map/all_to_all | solution.py:18
  46.0 5.3 %shard_map.102 = bf16[512,4096]{1,0:T(8,128)(2,1)} custom-call(s32[2]{0:T(128)S(1)} %copy-done.2, bf16[256,1152]{1,0:T(8,128)(2,1)S(1)} %reshape.416.first_ref, bf16[512,1024]{1,0:T(8,128)(2,1)S(1)} %multiply_convert_fusion.pool_ref), custom_call_target="tpu_custom_call" | custom-call | flops 1610612736 | bytes 8388608 | tf_op jit(solution)/shard_map/pallas_call | solution.py:143
  51.3 6.6 %all-to-all-start.1 = ((bf16[64,8,4096]{2,1,0:T(8,128)(2,1)}), bf16[64,8,4096]{2,1,0:T(8,128)(2,1)}, u32[]{:S(2)}, u32[]{:S(2)}) async-start(bf16[64,8,4096]{2,1,0:T(8,128)(2,1)} %bitcast.35), calls=%async_computation.1 | async-start | bytes 8388608 | tf_op jit(solution)/shard_map/all_to_all | solution.py:18
  58.6 2.3 reshape_reshape.3
  60.9 1.2 slice.113
  64.1 1.5 fusion.61
  65.6 0.7 fusion.89
  66.3 1.9 collective-permute-start.5
  68.2 1.4 collective-permute-start.4
  69.6 84.2 %all-to-all-done.1 = bf16[64,8,4096]{2,1,0:T(8,128)(2,1)} async-done(((bf16[64,8,4096]{2,1,0:T(8,128)(2,1)}), bf16[64,8,4096]{2,1,0:T(8,128)(2,1)}, u32[]{:S(2)}, u32[]{:S(2)}) %all-to-all-start.1) | async-done | bytes 4194336 | tf_op jit(solution)/shard_map/all_to_all | solution.py:18
  153.8 5.8 %shard_map.103 = (f32[64,1280]{1,0:T(8,128)S(1)}, s16[64,1280]{1,0:T(8,128)(2,1)S(1)}, s16[64,1280]{1,0:T(8,128)(2,1)S(1)}, s16[64,1280]{1,0:T(8,128)(2,1)S(1)}) custom-call(bf16[256,1024]{1,0:T(8,128)(2,1)S(1)} %fusion.24.q_ref.refs_7_, bf16[512,4096]{1,0:T(8,128)(2,1)} %bitcast.8.arrived_ref, s32[768,1]{1,0:T(8,128)S(1)} %fusion.33.code_ref), custom_call_target="tpu_custom_call" | custom-call | flops 2415919104 | bytes 8388608 | tf_op jit(solution)/shard_map/pallas_call | solution.py:191
  159.6 2.0 collective-permute-start.8
  161.6 1.4 collective-permute-start.7
  163.1 1.0 exponential_reduce_fusion.1
  164.0 1.3 collective-permute-done.8
  165.4 2.9 collective-permute-done.7
  168.3 4.5 %collective-permute-done.6 = s16[64,1280]{1,0:T(8,128)(2,1)S(1)} collective-permute-done((s16[64,1280]{1,0:T(8,128)(2,1)S(1)}, s16[64,1280]{1,0:T(8,128)(2,1)S(1)}, u32[]{:S(2)}, u32[]{:S(2)}) %collective-permute-start.6) | collective-permute-done | bytes 163872 | tf_op jit(solution)/shard_map/ppermute | solution.py:405
  173.5 1.5 collective-permute-start.19
  175.0 0.8 collective-permute-start.18
  176.4 2.6 collective-permute-start.13
  179.0 1.7 collective-permute-start.12
  181.4 3.7 %collective-permute-done.13.refs_2_ = bf16[64,1280]{1,0:T(8,128)(2,1)S(1)} collective-permute-done((bf16[64,1280]{1,0:T(8,128)(2,1)S(1)}, bf16[64,1280]{1,0:T(8,128)(2,1)S(1)}, u32[]{:S(2)}, u32[]{:S(2)}) %collective-permute-start.13) | collective-permute-done | bytes 163872 | tf_op jit(solution)/shard_map/ppermute | solution.py:422
  185.1 4.7 %shard_map.104 = bf16[512,4224]{1,0:T(8,128)(2,1)} custom-call(bf16[64,1280]{1,0:T(8,128)(2,1)S(1)} %get-tuple-element.23.refs_0_, bf16[64,1280]{1,0:T(8,128)(2,1)S(1)} %collective-permute-done.12.refs_1_, bf16[64,1280]{1,0:T(8,128)(2,1)S(1)} %collective-permute-done.13.refs_2_, bf16[64,1280]{1,0:T(8,128)(2,1)S(1)} %collective-permute-done.14.refs_3_, ...), custom_call_target="tpu_custom_call" | custom-call | flops 1879048192 | bytes 8388608 | tf_op jit(solution)/shard_map/pallas_call | solution.py:240
  189.8 8.6 %all-to-all-start.2 = ((bf16[64,8,4224]{2,1,0:T(8,128)(2,1)}), bf16[64,8,4224]{2,1,0:T(8,128)(2,1)}, u32[]{:S(2)}, u32[]{:S(2)}) async-start(bf16[64,8,4224]{2,1,0:T(8,128)(2,1)} %bitcast.34), calls=%async_computation.2 | async-start | bytes 8650752 | tf_op jit(solution)/shard_map/all_to_all | solution.py:18
  198.4 1.7 collective-permute-start.11
  200.1 2.2 collective-permute-start.10
  202.3 1.2 collective-permute-start.9
  203.6 1.1 fusion.1
  204.7 1.7 fusion.13
  206.4 1.7 fusion.15
  208.1 1.7 fusion.17
  209.8 1.7 fusion.11
  212.4 2.1 collective-permute-start.16
  214.8 1.0 copy-done.3
  220.9 76.3 %all-to-all-done.2 = bf16[64,8,4224]{2,1,0:T(8,128)(2,1)} async-done(((bf16[64,8,4224]{2,1,0:T(8,128)(2,1)}), bf16[64,8,4224]{2,1,0:T(8,128)(2,1)}, u32[]{:S(2)}, u32[]{:S(2)}) %all-to-all-start.2) | async-done | bytes 4325408 | tf_op jit(solution)/shard_map/all_to_all | solution.py:18
  297.1 1.8 shard_map.105
  299.0 1.0 all_to_all.30
  300.0 5.8 %all-to-all-start.3 = ((bf16[64,4,1152]{2,1,0:T(4,128)(2,1)}), bf16[64,4,1152]{2,1,0:T(4,128)(2,1)S(1)}, u32[]{:S(2)}, u32[]{:S(2)}) async-start(bf16[64,4,1152]{2,1,0:T(4,128)(2,1)} %all_to_all.30), calls=%async_computation.3 | async-start | bytes 1179648 | tf_op jit(solution)/shard_map/all_to_all | solution.py:18
  307.3 5.9 %shard_map.106 = bf16[512,1024]{1,0:T(8,128)(2,1)} custom-call(bf16[512,4224]{1,0:T(8,128)(2,1)} %bitcast.13.near_ref.extra_ref.third_ref, s32[3,512]{1,0:T(4,128)S(1)} %reshape.420.asked_ref, bf16[512,1024]{1,0:T(8,128)(2,1)S(1)} %copy-done, f32[512,1]{1,0:T(8,128)S(1)} %copy.34.inverse_ref, f32[1,1024]{1,0:T(1,128)S(1)} %bitcast.31), custom_call_target="tpu_custom_call" | custom-call | flops 1610612736 | bytes 8388608 | tf_op jit(solution)/shard_map/pallas_call | solution.py:310
  313.2 11.2 %all-to-all-done.3 = bf16[64,4,1152]{2,1,0:T(4,128)(2,1)S(1)} async-done(((bf16[64,4,1152]{2,1,0:T(4,128)(2,1)}), bf16[64,4,1152]{2,1,0:T(4,128)(2,1)S(1)}, u32[]{:S(2)}, u32[]{:S(2)}) %all-to-all-start.3) | async-done | bytes 589856 | tf_op jit(solution)/shard_map/all_to_all | solution.py:18
  324.7 1.1 fusion.10
  (107 shorter events, 11.4 us)
Async XLA Ops:
  0.6 9.8 %copy-start.12 = (s32[256,3]{0,1:T(4,128)S(1)}, s32[256,3]{0,1:T(4,128)}, u32[]{:S(2)}) copy-start(s32[256,3]{0,1:T(4,128)} %param.11) | copy-start | bytes 9220
  0.6 9.8 %copy-start.11 = (s32[32768]{0:T(1024)S(1)}, s32[32768]{0:T(1024)}, u32[]{:S(2)}) copy-start(s32[32768]{0:T(1024)} %param.12) | copy-start | bytes 393220
  2.3 10.2 %copy-start.1 = (f32[1024]{0:T(1024)S(1)}, f32[1024]{0:T(1024)}, u32[]{:S(2)}) copy-start(f32[1024]{0:T(1024)} %param.10) | copy-start | bytes 12292
  2.3 10.2 %copy-start.6 = (bf16[256,1024]{1,0:T(8,128)(2,1)S(1)}, bf16[256,1024]{1,0:T(8,128)(2,1)}, u32[]{:S(2)}) copy-start(bf16[256,1024]{1,0:T(8,128)(2,1)} %param.8) | copy-start | bytes 1572868
  3.9 8.4 %collective-permute-start.2 = (f32[1024]{0:T(1024)S(1)}, f32[1024]{0:T(1024)S(1)}, u32[]{:S(2)}, u32[]{:S(2)}) collective-permute-start(f32[1024]{0:T(1024)S(1)} %pad_maximum_fusion.5), channel_id=1, source_target_pairs={{0,3},{1,0},{2,1},{3,2},{4,7},{5,4},{6,5},{7,6},{8,11},{9,8},{10,9... | collective-permute-start | bytes 12296 | tf_op jit(solution)/shard_map/ppermute | solution.py:65
  7.6 4.8 %collective-permute-start.1 = (f32[1024]{0:T(1024)S(1)}, f32[1024]{0:T(1024)S(1)}, u32[]{:S(2)}, u32[]{:S(2)}) collective-permute-start(f32[1024]{0:T(1024)S(1)} %pad_maximum_fusion.5), channel_id=1, source_target_pairs={{0,2},{1,3},{2,0},{3,1},{4,6},{5,7},{6,4},{7,5},{8,10},{9,11},{10,... | collective-permute-start | bytes 12296 | tf_op jit(solution)/shard_map/ppermute | solution.py:65
  7.9 4.5 %collective-permute-start = (f32[1024]{0:T(1024)S(1)}, f32[1024]{0:T(1024)S(1)}, u32[]{:S(2)}, u32[]{:S(2)}) collective-permute-start(f32[1024]{0:T(1024)S(1)} %pad_maximum_fusion.5), channel_id=1, source_target_pairs={{0,1},{1,2},{2,3},{3,0},{4,5},{5,6},{6,7},{7,4},{8,9},{9,10},{10,1... | collective-permute-start | bytes 12296 | tf_op jit(solution)/shard_map/ppermute | solution.py:65
  12.4 14.7 %copy-start = (bf16[512,1024]{1,0:T(8,128)(2,1)S(1)}, bf16[512,1024]{1,0:T(8,128)(2,1)}, u32[]{:S(2)}) copy-start(bf16[512,1024]{1,0:T(8,128)(2,1)} %hidden_ref.1) | copy-start | bytes 3145732
  13.9 32.1 %copy-start.2 = (s32[2]{0:T(128)S(1)}, s32[2]{0:T(128)}, u32[]{:S(2)}) copy-start(s32[2]{0:T(128)} %masks_ref.1) | copy-start | bytes 28
  13.9 31.9 %all-to-all-start = ((bf16[64,4,1152]{2,1,0:T(4,128)(2,1)}), bf16[64,4,1152]{2,1,0:T(4,128)(2,1)S(1)}, u32[]{:S(2)}, u32[]{:S(2)}) async-start(bf16[64,4,1152]{2,1,0:T(4,128)(2,1)} %pad_maximum_fusion.1), calls=%async_computation | async-start | bytes 1179648 | tf_op jit(solution)/shard_map/all_to_all | solution.py:18
  45.8 5.5 %copy-start.9 = (bf16[64,4,1152]{2,1,0:T(4,128)(2,1)}, bf16[64,4,1152]{2,1,0:T(4,128)(2,1)S(1)}, u32[]{:S(2)}) copy-start(bf16[64,4,1152]{2,1,0:T(4,128)(2,1)S(1)} %all-to-all-done) | copy-start | bytes 1769476
  51.3 12.1 %copy-start.5 = (bf16[256,1024]{1,0:T(8,128)(2,1)S(1)}, bf16[256,1024]{1,0:T(8,128)(2,1)}, u32[]{:S(2)}) copy-start(bf16[256,1024]{1,0:T(8,128)(2,1)} %param.7) | copy-start | bytes 1572868
  51.3 102.5 %all-to-all-start.1 = ((bf16[64,8,4096]{2,1,0:T(8,128)(2,1)}), bf16[64,8,4096]{2,1,0:T(8,128)(2,1)}, u32[]{:S(2)}, u32[]{:S(2)}) async-start(bf16[64,8,4096]{2,1,0:T(8,128)(2,1)} %bitcast.35), calls=%async_computation.1 | async-start | bytes 8388608 | tf_op jit(solution)/shard_map/all_to_all | solution.py:18
  66.3 96.8 %collective-permute-start.5 = (f32[64,256]{1,0:T(8,128)}, f32[64,256]{1,0:T(8,128)S(1)}, u32[]{:S(2)}, u32[]{:S(2)}) collective-permute-start(f32[64,256]{1,0:T(8,128)} %get-tuple-element.25), channel_id=1, source_target_pairs={{0,3},{1,0},{2,1},{3,2},{4,7},{5,4},{6,5},{7,6},{8,11},{9,8},{10,9... | collective-permute-start | bytes 196616 | tf_op jit(solution)/shard_map/ppermute | solution.py:396
  68.2 94.8 %collective-permute-start.4 = (f32[64,256]{1,0:T(8,128)}, f32[64,256]{1,0:T(8,128)S(1)}, u32[]{:S(2)}, u32[]{:S(2)}) collective-permute-start(f32[64,256]{1,0:T(8,128)} %get-tuple-element.26), channel_id=1, source_target_pairs={{0,2},{1,3},{2,0},{3,1},{4,6},{5,7},{6,4},{7,5},{8,10},{9,11},{10,... | collective-permute-start | bytes 196616 | tf_op jit(solution)/shard_map/ppermute | solution.py:396
  69.6 93.4 %collective-permute-start.3 = (f32[64,256]{1,0:T(8,128)}, f32[64,256]{1,0:T(8,128)}, u32[]{:S(2)}, u32[]{:S(2)}) collective-permute-start(f32[64,256]{1,0:T(8,128)} %get-tuple-element.24), channel_id=1, source_target_pairs={{0,1},{1,2},{2,3},{3,0},{4,5},{5,6},{6,7},{7,4},{8,9},{9,10},{10,1... | collective-permute-start | bytes 196616 | tf_op jit(solution)/shard_map/ppermute | solution.py:396
  159.6 5.7 %collective-permute-start.8 = (s16[64,1280]{1,0:T(8,128)(2,1)S(1)}, s16[64,1280]{1,0:T(8,128)(2,1)S(1)}, u32[]{:S(2)}, u32[]{:S(2)}) collective-permute-start(s16[64,1280]{1,0:T(8,128)(2,1)S(1)} %get-tuple-element.11), channel_id=1, source_target_pairs={{0,3},{1,0},{2,1},{3,2},{4,7},{5,4},{6,5},{7,6},{8,11},{9,8},{10,9... | collective-permute-start | bytes 491528 | tf_op jit(solution)/shard_map/ppermute | solution.py:405
  161.6 6.6 %collective-permute-start.7 = (s16[64,1280]{1,0:T(8,128)(2,1)S(1)}, s16[64,1280]{1,0:T(8,128)(2,1)S(1)}, u32[]{:S(2)}, u32[]{:S(2)}) collective-permute-start(s16[64,1280]{1,0:T(8,128)(2,1)S(1)} %get-tuple-element.10), channel_id=1, source_target_pairs={{0,2},{1,3},{2,0},{3,1},{4,6},{5,7},{6,4},{7,5},{8,10},{9,11},{10,... | collective-permute-start | bytes 491528 | tf_op jit(solution)/shard_map/ppermute | solution.py:405
  163.0 9.7 %collective-permute-start.6 = (s16[64,1280]{1,0:T(8,128)(2,1)S(1)}, s16[64,1280]{1,0:T(8,128)(2,1)S(1)}, u32[]{:S(2)}, u32[]{:S(2)}) collective-permute-start(s16[64,1280]{1,0:T(8,128)(2,1)S(1)} %get-tuple-element.9), channel_id=1, source_target_pairs={{0,1},{1,2},{2,3},{3,0},{4,5},{5,6},{6,7},{7,4},{8,9},{9,10},{10,1... | collective-permute-start | bytes 491528 | tf_op jit(solution)/shard_map/ppermute | solution.py:405
  173.4 5.6 %collective-permute-start.20 = (f32[1536]{0:T(1024)S(1)}, f32[1536]{0:T(1024)S(1)}, u32[]{:S(2)}, u32[]{:S(2)}) collective-permute-start(f32[1536]{0:T(1024)S(1)} %maximum_multiply_fusion), channel_id=1, source_target_pairs={{0,3},{1,0},{2,1},{3,2},{4,7},{5,4},{6,5},{7,6},{8,11},{9,8},{10,9... | collective-permute-start | bytes 18440 | tf_op jit(solution)/shard_map/ppermute | solution.py:65
  173.5 7.2 %collective-permute-start.19 = (f32[1536]{0:T(1024)S(1)}, f32[1536]{0:T(1024)S(1)}, u32[]{:S(2)}, u32[]{:S(2)}) collective-permute-start(f32[1536]{0:T(1024)S(1)} %maximum_multiply_fusion), channel_id=1, source_target_pairs={{0,2},{1,3},{2,0},{3,1},{4,6},{5,7},{6,4},{7,5},{8,10},{9,11},{10,... | collective-permute-start | bytes 18440 | tf_op jit(solution)/shard_map/ppermute | solution.py:65
  175.0 5.7 %collective-permute-start.18 = (f32[1536]{0:T(1024)S(1)}, f32[1536]{0:T(1024)S(1)}, u32[]{:S(2)}, u32[]{:S(2)}) collective-permute-start(f32[1536]{0:T(1024)S(1)} %maximum_multiply_fusion), channel_id=1, source_target_pairs={{0,1},{1,2},{2,3},{3,0},{4,5},{5,6},{6,7},{7,4},{8,9},{9,10},{10,1... | collective-permute-start | bytes 18440 | tf_op jit(solution)/shard_map/ppermute | solution.py:65
  175.8 5.5 %collective-permute-start.14 = (bf16[64,1280]{1,0:T(8,128)(2,1)S(1)}, bf16[64,1280]{1,0:T(8,128)(2,1)S(1)}, u32[]{:S(2)}, u32[]{:S(2)}) collective-permute-start(bf16[64,1280]{1,0:T(8,128)(2,1)S(1)} %get-tuple-element.23.refs_0_), channel_id=1, source_target_pairs={{3,0},{0,1},{1,2},{2,3},{7,4},{4,5},{5,6},{6,7},{11,8},{8,9},{9,10... | collective-permute-start | bytes 491528 | tf_op jit(solution)/shard_map/ppermute | solution.py:422
  176.4 8.7 %collective-permute-start.13 = (bf16[64,1280]{1,0:T(8,128)(2,1)S(1)}, bf16[64,1280]{1,0:T(8,128)(2,1)S(1)}, u32[]{:S(2)}, u32[]{:S(2)}) collective-permute-start(bf16[64,1280]{1,0:T(8,128)(2,1)S(1)} %get-tuple-element.23.refs_0_), channel_id=1, source_target_pairs={{2,0},{3,1},{0,2},{1,3},{6,4},{7,5},{4,6},{5,7},{10,8},{11,9},{8,1... | collective-permute-start | bytes 491528 | tf_op jit(solution)/shard_map/ppermute | solution.py:422
  179.0 6.1 %collective-permute-start.12 = (bf16[64,1280]{1,0:T(8,128)(2,1)S(1)}, bf16[64,1280]{1,0:T(8,128)(2,1)S(1)}, u32[]{:S(2)}, u32[]{:S(2)}) collective-permute-start(bf16[64,1280]{1,0:T(8,128)(2,1)S(1)} %get-tuple-element.23.refs_0_), channel_id=1, source_target_pairs={{1,0},{2,1},{3,2},{0,3},{5,4},{6,5},{7,6},{4,7},{9,8},{10,9},{11,1... | collective-permute-start | bytes 491528 | tf_op jit(solution)/shard_map/ppermute | solution.py:422
  189.8 107.3 %all-to-all-start.2 = ((bf16[64,8,4224]{2,1,0:T(8,128)(2,1)}), bf16[64,8,4224]{2,1,0:T(8,128)(2,1)}, u32[]{:S(2)}, u32[]{:S(2)}) async-start(bf16[64,8,4224]{2,1,0:T(8,128)(2,1)} %bitcast.34), calls=%async_computation.2 | async-start | bytes 8650752 | tf_op jit(solution)/shard_map/all_to_all | solution.py:18
  198.4 13.1 %collective-permute-start.11 = (bf16[64,256]{1,0:T(8,128)(2,1)S(1)}, bf16[64,256]{1,0:T(8,128)(2,1)S(1)}, u32[]{:S(2)}, u32[]{:S(2)}) collective-permute-start(bf16[64,256]{1,0:T(8,128)(2,1)S(1)} %get-tuple-element.31), channel_id=1, source_target_pairs={{3,0},{0,1},{1,2},{2,3},{7,4},{4,5},{5,6},{6,7},{11,8},{8,9},{9,10... | collective-permute-start | bytes 98312 | tf_op jit(solution)/shard_map/ppermute | solution.py:422
  200.1 11.4 %collective-permute-start.10 = (bf16[64,256]{1,0:T(8,128)(2,1)S(1)}, bf16[64,256]{1,0:T(8,128)(2,1)S(1)}, u32[]{:S(2)}, u32[]{:S(2)}) collective-permute-start(bf16[64,256]{1,0:T(8,128)(2,1)S(1)} %get-tuple-element.31), channel_id=1, source_target_pairs={{2,0},{3,1},{0,2},{1,3},{6,4},{7,5},{4,6},{5,7},{10,8},{11,9},{8,1... | collective-permute-start | bytes 98312 | tf_op jit(solution)/shard_map/ppermute | solution.py:422
  202.3 9.2 %collective-permute-start.9 = (bf16[64,256]{1,0:T(8,128)(2,1)S(1)}, bf16[64,256]{1,0:T(8,128)(2,1)S(1)}, u32[]{:S(2)}, u32[]{:S(2)}) collective-permute-start(bf16[64,256]{1,0:T(8,128)(2,1)S(1)} %get-tuple-element.31), channel_id=1, source_target_pairs={{1,0},{2,1},{3,2},{0,3},{5,4},{6,5},{7,6},{4,7},{9,8},{10,9},{11,1... | collective-permute-start | bytes 98312 | tf_op jit(solution)/shard_map/ppermute | solution.py:422
  208.1 3.5 %copy-start.7 = (bf16[256,1024]{1,0:T(8,128)(2,1)S(1)}, bf16[256,1024]{1,0:T(8,128)(2,1)}, u32[]{:S(2)}) copy-start(bf16[256,1024]{1,0:T(8,128)(2,1)} %param.8) | copy-start | bytes 1572868
  212.3 5.5 %collective-permute-start.17 = (f32[256]{0:T(256)S(1)}, f32[256]{0:T(256)S(1)}, u32[]{:S(2)}, u32[]{:S(2)}) collective-permute-start(f32[256]{0:T(256)S(1)} %multiply_reduce_fusion.1), channel_id=1, source_target_pairs={{0,3},{1,0},{2,1},{3,2},{4,7},{5,4},{6,5},{7,6},{8,11},{9,8},{10,9... | collective-permute-start | bytes 3080 | tf_op jit(solution)/shard_map/ppermute | solution.py:65
  212.4 5.4 %collective-permute-start.16 = (f32[256]{0:T(256)S(1)}, f32[256]{0:T(256)S(1)}, u32[]{:S(2)}, u32[]{:S(2)}) collective-permute-start(f32[256]{0:T(256)S(1)} %multiply_reduce_fusion.1), channel_id=1, source_target_pairs={{0,2},{1,3},{2,0},{3,1},{4,6},{5,7},{6,4},{7,5},{8,10},{9,11},{10,... | collective-permute-start | bytes 3080 | tf_op jit(solution)/shard_map/ppermute | solution.py:65
  214.4 4.0 %collective-permute-start.15 = (f32[256]{0:T(256)S(1)}, f32[256]{0:T(256)S(1)}, u32[]{:S(2)}, u32[]{:S(2)}) collective-permute-start(f32[256]{0:T(256)S(1)} %multiply_reduce_fusion.1), channel_id=1, source_target_pairs={{0,1},{1,2},{2,3},{3,0},{4,5},{5,6},{6,7},{7,4},{8,9},{9,10},{10,1... | collective-permute-start | bytes 3080 | tf_op jit(solution)/shard_map/ppermute | solution.py:65
  214.8 1.0 copy-start.3
  218.9 2.0 copy-start.10
  300.0 24.5 %all-to-all-start.3 = ((bf16[64,4,1152]{2,1,0:T(4,128)(2,1)}), bf16[64,4,1152]{2,1,0:T(4,128)(2,1)S(1)}, u32[]{:S(2)}, u32[]{:S(2)}) async-start(bf16[64,4,1152]{2,1,0:T(4,128)(2,1)} %all_to_all.30), calls=%async_computation.3 | async-start | bytes 1179648 | tf_op jit(solution)/shard_map/all_to_all | solution.py:18
  313.2 11.4 %copy-start.4 = (f32[256,1024]{1,0:T(8,128)S(1)}, f32[256,1024]{1,0:T(8,128)}, u32[]{:S(2)}) copy-start(f32[256,1024]{1,0:T(8,128)} %copy-done.3) | copy-start | bytes 3145732
  313.2 11.5 %copy-start.8 = (bf16[256,1024]{1,0:T(8,128)(2,1)S(1)}, bf16[256,1024]{1,0:T(8,128)(2,1)}, u32[]{:S(2)}) copy-start(bf16[256,1024]{1,0:T(8,128)(2,1)} %param.8) | copy-start | bytes 1572868

commit v2 on v1

--- a/solution.py
+++ b/solution.py
@@ -55,7 +55,15 @@
 
 
 def after(x, value):
-    return jnp.where(jnp.isnan(value.reshape(-1)[0].astype(F32)), jnp.zeros_like(x), x)
+    corner = lax.slice(value, (0,) * value.ndim, (1,) * value.ndim).astype(F32)
+    return jnp.where(jnp.isnan(corner).reshape((1,) * x.ndim), jnp.zeros_like(x), x)
+
+
+def folded(x):
+    parts = lax.axis_size("mp")
+    for bit in range(parts.bit_length() - 1):
+        x = x + lax.ppermute(x, "mp", [(i, i ^ 1 << bit) for i in range(parts)])
+    return x
 
 
 def summed(x):
@@ -339,14 +347,11 @@
     share = rows_dev // parts
     int_range = lambda n: jnp.arange(n, dtype=jnp.int32)
 
-    partial_squares = jnp.concatenate(
-        [row_squares(x, norm_gain) for x in (positive_hidden, query_hidden, pool_hidden)]
-    )
-    inverse = lax.rsqrt(summed(partial_squares) + EPSILON)
-    inverse_p, inverse_q, inverse_pool = jnp.split(inverse, [rows_dev, 2 * rows_dev])
+    partial_squares = row_squares(positive_hidden, norm_gain)
+    inverse_p = lax.rsqrt(summed(partial_squares) + EPSILON)
     emb_p = embedding(positive_hidden, norm_gain, inverse_p)
 
-    ids = after(hard_ids, partial_squares).T.reshape(-1)
+    ids = jnp.where(partial_squares[:, None] < 0.0, 0, hard_ids).T.reshape(-1)
     storage = looked_up(location, ids)
     owners = storage // pool_dev
     local_row = storage % pool_dev
@@ -367,15 +372,16 @@
     request_line = one_hot(owners * chunk + line % chunk, devices * chunk)
     requests = dot(request_line, digits, ((0,), (0,))).astype(BF)
 
-    first = exchanged(
-        jnp.concatenate(
-            [
-                emb_p.reshape(devices, chunk, feature_dev),
-                requests.reshape(devices, chunk, 128),
-            ],
-            axis=2,
-        )
-    ).reshape(rows_dev, feature_dev + 128)
+    packed = jnp.concatenate(
+        [emb_p.reshape(devices, chunk, feature_dev), requests.reshape(devices, chunk, 128)], axis=2
+    )
+    first = exchanged(packed).reshape(rows_dev, feature_dev + 128)
+    tie = packed[0, 0, 128:].astype(F32)
+    late_gain = jnp.where(jnp.isnan(tie), 0.0, norm_gain)
+    squares = lax.psum(
+        jnp.concatenate([row_squares(x, late_gain) for x in (query_hidden, pool_hidden)]), "mp"
+    )
+    inverse_q, inverse_pool = jnp.split(lax.rsqrt(squares + EPSILON), [rows_dev])
     halves = GROUP // chunk
     asked = first[:, feature_dev:].reshape(devices, chunk, 128).astype(jnp.int32)
     asked = asked[:, :, : steps * halves] * 16 + asked[:, :, 64 : 64 + steps * halves] - 1
@@ -424,7 +430,7 @@
         return pieces
 
     far_pieces = gathered(weights_far)
-    values = summed(
+    values = folded(
         jnp.concatenate(
             [
                 jnp.sum(weights_far.astype(F32) * scores_far, axis=0),

time: 327 us -> 325 us (level)
  blocking collectives: 0 us -> 8.54 us
  waiting for transfers between devices: 204 us -> 199 us
  starting transfers between devices: 60.1 us -> 56.8 us
    psum x0 -> x1, blocking collectives: none -> 8.54 us  [per_device(): lax.psum(jnp.concatenate([row_squares(x, late_gain) for x in (query_hidde...]
    all_to_all x4, waiting for transfers between devices: 190 us -> 184 us  [exchanged(): return lax.all_to_all(x, 'batch', split_axis=0, concat_axis=0, tiled=True)]
    ppermute x0 -> x2, waiting for transfers between devices: none -> 4.77 us  [folded(): x = x + lax.ppermute(x, 'mp', [(i, i ^ 1 << bit) for i in range(parts)])]
    ppermute x6, waiting for transfers between devices: 4.26 us -> 0.35 us  [gathered(): lax.ppermute(piece, 'mp', [((i + step) % parts, i) for i in range(parts)])]
    ppermute x9 -> x6, starting transfers between devices: 9.16 us -> 7.73 us  [summed(): lax.ppermute(x, 'mp', [(i, (i + step) % parts) for i in range(parts)])]
  transfers between devices with their start and end apart: 25 -> 24, of which waited for: 10 -> 10; matrix products, arithmetic and copies ran while one was open for 7% -> 7% of each run, Pallas kernels for 4% -> 4%
where the time goes in v2:
time: 325 us; the launch traced here: 324 us
  waiting for transfers between devices  199 us (61%)
  starting transfers between devices  56.8 us (17%)
  Pallas kernels  23.6 us (7%)
  matrix products  11.5 us (4%)
  other arithmetic  11.3 us (3%)
  blocking collectives  8.54 us (3%)
  local copies, waits for them, and re-layouts  8.33 us (3%)
  between operations  5.12 us (2%)
    all_to_all x4, waiting for transfers between devices, exchanged(): return lax.all_to_all(x, 'batch', split_axis=0, concat_axis=0, tiled=True)  184 us
    all_to_all x4, starting transfers between devices, exchanged(): return lax.all_to_all(x, 'batch', split_axis=0, concat_axis=0, tiled=True)  33.3 us
    dot_general x10, matrix products, dot(): return lax.dot_general(a, b, (dims, ((), ())), preferred_element_type=F32)  11.5 us
    ppermute x3, waiting for transfers between devices, per_device(): lax.ppermute(coded[step - 1], 'mp', [(i, (i + step) % parts) for i in ran...  8.73 us
    psum x1, blocking collectives, per_device(): lax.psum(jnp.concatenate([row_squares(x, late_gain) for x in (query_hidde...  8.54 us
    ppermute x6, starting transfers between devices, gathered(): lax.ppermute(piece, 'mp', [((i + step) % parts, i) for i in range(parts)])  7.94 us
    ppermute x6, starting transfers between devices, summed(): lax.ppermute(x, 'mp', [(i, (i + step) % parts) for i in range(parts)])  7.73 us
  transfers between devices with their start and end apart: 24, of which 10 were waited for; matrix products, arithmetic and copies ran while one was open for 7% of the time, Pallas kernels for 4%

profile of v2, /device:TPU:1, one launch (start us, length us, event | category | flops | bytes accessed | tf_op | source)
XLA Modules:
  0.0 323.9 jit_solution(10737027974717461203)
XLA Ops:
  0.7 1.3 multiply_reduce_fusion
  2.0 3.6 %collective-permute-start.2 = (f32[256]{0:T(256)S(1)}, f32[256]{0:T(256)S(1)}, u32[]{:S(2)}, u32[]{:S(2)}) collective-permute-start(f32[256]{0:T(256)S(1)} %multiply_reduce_fusion), channel_id=1, source_target_pairs={{0,3},{1,0},{2,1},{3,2},{4,7},{5,4},{6,5},{7,6},{8,11},{9,8},{10,9... | collective-permute-start | bytes 3080 | tf_op jit(solution)/shard_map/ppermute | solution.py:73
  6.7 0.7 and_bitcast_fusion
  7.4 0.9 fusion.79
  9.2 0.9 convolution_convert_fusion
  10.7 1.1 pad_maximum_fusion
  11.8 13.4 %all-to-all-start = ((bf16[64,4,1152]{2,1,0:T(4,128)(2,1)}), bf16[64,4,1152]{2,1,0:T(4,128)(2,1)}, u32[]{:S(2)}, u32[]{:S(2)}) async-start(bf16[64,4,1152]{2,1,0:T(4,128)(2,1)} %pad_maximum_fusion), calls=%async_computation | async-start | bytes 1179648 | tf_op jit(solution)/shard_map/all_to_all | solution.py:18
  25.8 8.5 %psum.7 = f32[768]{0:T(1024)S(1)} all-reduce(f32[768]{0:T(1024)S(1)} %pad_maximum_fusion.5), channel_id=1, replica_groups=mesh['batch'=64,'mp'=4] {'mp'}, use_global_device_ids=true, to_apply=%region_5.6 | all-reduce | flops 768 | bytes 6144 | tf_op jit(solution)/shard_map/psum | solution.py:381
  34.6 9.2 %all-to-all-done = bf16[64,4,1152]{2,1,0:T(4,128)(2,1)} async-done(((bf16[64,4,1152]{2,1,0:T(4,128)(2,1)}), bf16[64,4,1152]{2,1,0:T(4,128)(2,1)}, u32[]{:S(2)}, u32[]{:S(2)}) %all-to-all-start) | async-done | bytes 589856 | tf_op jit(solution)/shard_map/all_to_all | solution.py:18
  43.8 1.5 reshape.417.first_ref
  45.3 5.4 %shard_map.102 = bf16[512,4096]{1,0:T(8,128)(2,1)} custom-call(s32[2]{0:T(128)S(1)} %copy-done.2, bf16[256,1152]{1,0:T(8,128)(2,1)S(1)} %reshape.417.first_ref, bf16[512,1024]{1,0:T(8,128)(2,1)S(1)} %fusion.7.pool_ref), custom_call_target="tpu_custom_call" | custom-call | flops 1610612736 | bytes 8388608 | tf_op jit(solution)/shard_map/pallas_call | solution.py:151
  50.7 6.5 %all-to-all-start.1 = ((bf16[64,8,4096]{2,1,0:T(8,128)(2,1)}), bf16[64,8,4096]{2,1,0:T(8,128)(2,1)}, u32[]{:S(2)}, u32[]{:S(2)}) async-start(bf16[64,8,4096]{2,1,0:T(8,128)(2,1)} %bitcast.29), calls=%async_computation.1 | async-start | bytes 8388608 | tf_op jit(solution)/shard_map/all_to_all | solution.py:18
  60.4 1.5 fusion.75
  62.6 1.7 collective-permute-start.5
  64.3 1.4 collective-permute-start.4
  65.7 87.3 %all-to-all-done.1 = bf16[64,8,4096]{2,1,0:T(8,128)(2,1)} async-done(((bf16[64,8,4096]{2,1,0:T(8,128)(2,1)}), bf16[64,8,4096]{2,1,0:T(8,128)(2,1)}, u32[]{:S(2)}, u32[]{:S(2)}) %all-to-all-start.1) | async-done | bytes 4194336 | tf_op jit(solution)/shard_map/all_to_all | solution.py:18
  153.0 5.8 %shard_map.103 = (f32[64,1280]{1,0:T(8,128)S(1)}, s16[64,1280]{1,0:T(8,128)(2,1)S(1)}, s16[64,1280]{1,0:T(8,128)(2,1)S(1)}, s16[64,1280]{1,0:T(8,128)(2,1)S(1)}) custom-call(bf16[256,1024]{1,0:T(8,128)(2,1)S(1)} %fusion.38.q_ref.refs_7_, bf16[512,4096]{1,0:T(8,128)(2,1)} %bitcast.7.arrived_ref, s32[768,1]{1,0:T(8,128)S(1)} %fusion.47.code_ref), custom_call_target="tpu_custom_call" | custom-call | flops 2415919104 | bytes 8388608 | tf_op jit(solution)/shard_map/pallas_call | solution.py:199
  158.8 1.8 collective-permute-start.8
  160.6 1.4 collective-permute-start.7
  162.1 1.0 exponential_reduce_fusion.1
  163.0 1.3 collective-permute-done.8
  164.3 2.9 collective-permute-done.7
  167.3 4.5 %collective-permute-done.6 = s16[64,1280]{1,0:T(8,128)(2,1)S(1)} collective-permute-done((s16[64,1280]{1,0:T(8,128)(2,1)S(1)}, s16[64,1280]{1,0:T(8,128)(2,1)S(1)}, u32[]{:S(2)}, u32[]{:S(2)}) %collective-permute-start.6) | collective-permute-done | bytes 163872 | tf_op jit(solution)/shard_map/ppermute | solution.py:411
  172.5 1.5 collective-permute-start.14
  174.0 1.4 collective-permute-start.13
  175.4 1.0 collective-permute-start.12
  176.4 1.4 collective-permute-start.19
  177.8 4.8 %collective-permute-done.19 = f32[1536]{0:T(1024)S(1)} collective-permute-done((f32[1536]{0:T(1024)S(1)}, f32[1536]{0:T(1024)S(1)}, u32[]{:S(2)}, u32[]{:S(2)}) %collective-permute-start.19) | collective-permute-done | bytes 6176 | tf_op jit(solution)/shard_map/ppermute | solution.py:65
  182.9 4.7 %shard_map.104 = bf16[512,4224]{1,0:T(8,128)(2,1)} custom-call(bf16[64,1280]{1,0:T(8,128)(2,1)S(1)} %get-tuple-element.21.refs_0_, bf16[64,1280]{1,0:T(8,128)(2,1)S(1)} %collective-permute-done.12.refs_1_, bf16[64,1280]{1,0:T(8,128)(2,1)S(1)} %collective-permute-done.13.refs_2_, bf16[64,1280]{1,0:T(8,128)(2,1)S(1)} %collective-permute-done.14.refs_3_, ...), custom_call_target="tpu_custom_call" | custom-call | flops 1879048192 | bytes 8388608 | tf_op jit(solution)/shard_map/pallas_call | solution.py:248
  187.7 7.4 %all-to-all-start.2 = ((bf16[64,8,4224]{2,1,0:T(8,128)(2,1)}), bf16[64,8,4224]{2,1,0:T(8,128)(2,1)}, u32[]{:S(2)}, u32[]{:S(2)}) async-start(bf16[64,8,4224]{2,1,0:T(8,128)(2,1)} %bitcast.28), calls=%async_computation.2 | async-start | bytes 8650752 | tf_op jit(solution)/shard_map/all_to_all | solution.py:18
  195.1 1.4 collective-permute-start.11
  196.5 2.4 collective-permute-start.10
  199.3 1.1 fusion.1
  200.4 1.7 fusion.27
  202.1 1.7 fusion.29
  203.8 1.7 fusion.31
  205.5 1.7 fusion.25
  208.6 2.4 collective-permute-start.16
  211.4 1.1 copy-done.7
  214.3 0.8 collective-permute-done.15
  217.4 76.4 %all-to-all-done.2 = bf16[64,8,4224]{2,1,0:T(8,128)(2,1)} async-done(((bf16[64,8,4224]{2,1,0:T(8,128)(2,1)}), bf16[64,8,4224]{2,1,0:T(8,128)(2,1)}, u32[]{:S(2)}, u32[]{:S(2)}) %all-to-all-start.2) | async-done | bytes 4325408 | tf_op jit(solution)/shard_map/all_to_all | solution.py:18
  293.8 1.8 shard_map.105
  295.7 1.0 all_to_all.30
  296.6 5.9 %all-to-all-start.3 = ((bf16[64,4,1152]{2,1,0:T(4,128)(2,1)}), bf16[64,4,1152]{2,1,0:T(4,128)(2,1)}, u32[]{:S(2)}, u32[]{:S(2)}) async-start(bf16[64,4,1152]{2,1,0:T(4,128)(2,1)} %all_to_all.30), calls=%async_computation.3 | async-start | bytes 1179648 | tf_op jit(solution)/shard_map/all_to_all | solution.py:18
  304.1 5.9 %shard_map.106 = bf16[512,1024]{1,0:T(8,128)(2,1)} custom-call(bf16[512,4224]{1,0:T(8,128)(2,1)} %bitcast.12.near_ref.extra_ref.third_ref, s32[3,512]{1,0:T(4,128)S(1)} %reshape.419.asked_ref, bf16[512,1024]{1,0:T(8,128)(2,1)S(1)} %copy-done, f32[512,1]{1,0:T(8,128)S(1)} %copy.34.inverse_ref, f32[1,1024]{1,0:T(1,128)S(1)} %bitcast.26), custom_call_target="tpu_custom_call" | custom-call | flops 1610612736 | bytes 8388608 | tf_op jit(solution)/shard_map/pallas_call | solution.py:318
  310.1 11.2 %all-to-all-done.3 = bf16[64,4,1152]{2,1,0:T(4,128)(2,1)} async-done(((bf16[64,4,1152]{2,1,0:T(4,128)(2,1)}), bf16[64,4,1152]{2,1,0:T(4,128)(2,1)}, u32[]{:S(2)}, u32[]{:S(2)}) %all-to-all-start.3) | async-done | bytes 589856 | tf_op jit(solution)/shard_map/all_to_all | solution.py:18
  321.2 1.4 reshape.420
  322.8 1.2 fusion.24
  (102 shorter events, 12.2 us)
Async XLA Ops:
  0.6 9.6 %copy-start.4 = (bf16[256,1024]{1,0:T(8,128)(2,1)S(1)}, bf16[256,1024]{1,0:T(8,128)(2,1)}, u32[]{:S(2)}) copy-start(bf16[256,1024]{1,0:T(8,128)(2,1)} %param.8) | copy-start | bytes 1572868
  0.6 9.6 %copy-start.1 = (f32[1024]{0:T(1024)S(1)}, f32[1024]{0:T(1024)}, u32[]{:S(2)}) copy-start(f32[1024]{0:T(1024)} %param.10) | copy-start | bytes 12292
  2.0 8.2 %collective-permute-start.2 = (f32[256]{0:T(256)S(1)}, f32[256]{0:T(256)S(1)}, u32[]{:S(2)}, u32[]{:S(2)}) collective-permute-start(f32[256]{0:T(256)S(1)} %multiply_reduce_fusion), channel_id=1, source_target_pairs={{0,3},{1,0},{2,1},{3,2},{4,7},{5,4},{6,5},{7,6},{8,11},{9,8},{10,9... | collective-permute-start | bytes 3080 | tf_op jit(solution)/shard_map/ppermute | solution.py:73
  5.6 4.6 %collective-permute-start.1 = (f32[256]{0:T(256)S(1)}, f32[256]{0:T(256)S(1)}, u32[]{:S(2)}, u32[]{:S(2)}) collective-permute-start(f32[256]{0:T(256)S(1)} %multiply_reduce_fusion), channel_id=1, source_target_pairs={{0,2},{1,3},{2,0},{3,1},{4,6},{5,7},{6,4},{7,5},{8,10},{9,11},{10,... | collective-permute-start | bytes 3080 | tf_op jit(solution)/shard_map/ppermute | solution.py:73
  6.0 4.2 %collective-permute-start = (f32[256]{0:T(256)S(1)}, f32[256]{0:T(256)S(1)}, u32[]{:S(2)}, u32[]{:S(2)}) collective-permute-start(f32[256]{0:T(256)S(1)} %multiply_reduce_fusion), channel_id=1, source_target_pairs={{0,1},{1,2},{2,3},{3,0},{4,5},{5,6},{6,7},{7,4},{8,9},{9,10},{10,1... | collective-permute-start | bytes 3080 | tf_op jit(solution)/shard_map/ppermute | solution.py:73
  10.4 14.8 %copy-start.3 = (bf16[256,1024]{1,0:T(8,128)(2,1)S(1)}, bf16[256,1024]{1,0:T(8,128)(2,1)}, u32[]{:S(2)}) copy-start(bf16[256,1024]{1,0:T(8,128)(2,1)} %param.7) | copy-start | bytes 1572868
  10.4 15.0 %copy-start = (bf16[512,1024]{1,0:T(8,128)(2,1)S(1)}, bf16[512,1024]{1,0:T(8,128)(2,1)}, u32[]{:S(2)}) copy-start(bf16[512,1024]{1,0:T(8,128)(2,1)} %hidden_ref.1) | copy-start | bytes 3145732
  11.8 32.1 %all-to-all-start = ((bf16[64,4,1152]{2,1,0:T(4,128)(2,1)}), bf16[64,4,1152]{2,1,0:T(4,128)(2,1)}, u32[]{:S(2)}, u32[]{:S(2)}) async-start(bf16[64,4,1152]{2,1,0:T(4,128)(2,1)} %pad_maximum_fusion), calls=%async_computation | async-start | bytes 1179648 | tf_op jit(solution)/shard_map/all_to_all | solution.py:18
  25.4 19.9 %copy-start.2 = (s32[2]{0:T(128)S(1)}, s32[2]{0:T(128)}, u32[]{:S(2)}) copy-start(s32[2]{0:T(128)} %masks_ref.1) | copy-start | bytes 28
  50.7 102.4 %all-to-all-start.1 = ((bf16[64,8,4096]{2,1,0:T(8,128)(2,1)}), bf16[64,8,4096]{2,1,0:T(8,128)(2,1)}, u32[]{:S(2)}, u32[]{:S(2)}) async-start(bf16[64,8,4096]{2,1,0:T(8,128)(2,1)} %bitcast.29), calls=%async_computation.1 | async-start | bytes 8388608 | tf_op jit(solution)/shard_map/all_to_all | solution.py:18
  62.6 99.5 %collective-permute-start.5 = (f32[64,256]{1,0:T(8,128)}, f32[64,256]{1,0:T(8,128)S(1)}, u32[]{:S(2)}, u32[]{:S(2)}) collective-permute-start(f32[64,256]{1,0:T(8,128)} %get-tuple-element.23), channel_id=1, source_target_pairs={{0,3},{1,0},{2,1},{3,2},{4,7},{5,4},{6,5},{7,6},{8,11},{9,8},{10,9... | collective-permute-start | bytes 196616 | tf_op jit(solution)/shard_map/ppermute | solution.py:402
  64.3 97.7 %collective-permute-start.4 = (f32[64,256]{1,0:T(8,128)}, f32[64,256]{1,0:T(8,128)S(1)}, u32[]{:S(2)}, u32[]{:S(2)}) collective-permute-start(f32[64,256]{1,0:T(8,128)} %get-tuple-element.24), channel_id=1, source_target_pairs={{0,2},{1,3},{2,0},{3,1},{4,6},{5,7},{6,4},{7,5},{8,10},{9,11},{10,... | collective-permute-start | bytes 196616 | tf_op jit(solution)/shard_map/ppermute | solution.py:402
  65.7 96.3 %collective-permute-start.3 = (f32[64,256]{1,0:T(8,128)}, f32[64,256]{1,0:T(8,128)}, u32[]{:S(2)}, u32[]{:S(2)}) collective-permute-start(f32[64,256]{1,0:T(8,128)} %get-tuple-element.22), channel_id=1, source_target_pairs={{0,1},{1,2},{2,3},{3,0},{4,5},{5,6},{6,7},{7,4},{8,9},{9,10},{10,1... | collective-permute-start | bytes 196616 | tf_op jit(solution)/shard_map/ppermute | solution.py:402
  158.8 5.5 %collective-permute-start.8 = (s16[64,1280]{1,0:T(8,128)(2,1)S(1)}, s16[64,1280]{1,0:T(8,128)(2,1)S(1)}, u32[]{:S(2)}, u32[]{:S(2)}) collective-permute-start(s16[64,1280]{1,0:T(8,128)(2,1)S(1)} %get-tuple-element.11), channel_id=1, source_target_pairs={{0,3},{1,0},{2,1},{3,2},{4,7},{5,4},{6,5},{7,6},{8,11},{9,8},{10,9... | collective-permute-start | bytes 491528 | tf_op jit(solution)/shard_map/ppermute | solution.py:411
  160.6 6.6 %collective-permute-start.7 = (s16[64,1280]{1,0:T(8,128)(2,1)S(1)}, s16[64,1280]{1,0:T(8,128)(2,1)S(1)}, u32[]{:S(2)}, u32[]{:S(2)}) collective-permute-start(s16[64,1280]{1,0:T(8,128)(2,1)S(1)} %get-tuple-element.10), channel_id=1, source_target_pairs={{0,2},{1,3},{2,0},{3,1},{4,6},{5,7},{6,4},{7,5},{8,10},{9,11},{10,... | collective-permute-start | bytes 491528 | tf_op jit(solution)/shard_map/ppermute | solution.py:411
  162.0 9.7 %collective-permute-start.6 = (s16[64,1280]{1,0:T(8,128)(2,1)S(1)}, s16[64,1280]{1,0:T(8,128)(2,1)S(1)}, u32[]{:S(2)}, u32[]{:S(2)}) collective-permute-start(s16[64,1280]{1,0:T(8,128)(2,1)S(1)} %get-tuple-element.9), channel_id=1, source_target_pairs={{0,1},{1,2},{2,3},{3,0},{4,5},{5,6},{6,7},{7,4},{8,9},{9,10},{10,1... | collective-permute-start | bytes 491528 | tf_op jit(solution)/shard_map/ppermute | solution.py:411
  172.4 4.0 %collective-permute-start.18 = (f32[1536]{0:T(1024)S(1)}, f32[1536]{0:T(1024)S(1)}, u32[]{:S(2)}, u32[]{:S(2)}) collective-permute-start(f32[1536]{0:T(1024)S(1)} %maximum_multiply_fusion), channel_id=1, source_target_pairs={{0,1},{1,0},{2,3},{3,2},{4,5},{5,4},{6,7},{7,6},{8,9},{9,8},{10,11... | collective-permute-start | bytes 18440 | tf_op jit(solution)/shard_map/ppermute | solution.py:65
  172.5 10.1 %collective-permute-start.14 = (bf16[64,1280]{1,0:T(8,128)(2,1)S(1)}, bf16[64,1280]{1,0:T(8,128)(2,1)S(1)}, u32[]{:S(2)}, u32[]{:S(2)}) collective-permute-start(bf16[64,1280]{1,0:T(8,128)(2,1)S(1)} %get-tuple-element.21.refs_0_), channel_id=1, source_target_pairs={{3,0},{0,1},{1,2},{2,3},{7,4},{4,5},{5,6},{6,7},{11,8},{8,9},{9,10... | collective-permute-start | bytes 491528 | tf_op jit(solution)/shard_map/ppermute | solution.py:428
  174.0 8.6 %collective-permute-start.13 = (bf16[64,1280]{1,0:T(8,128)(2,1)S(1)}, bf16[64,1280]{1,0:T(8,128)(2,1)S(1)}, u32[]{:S(2)}, u32[]{:S(2)}) collective-permute-start(bf16[64,1280]{1,0:T(8,128)(2,1)S(1)} %get-tuple-element.21.refs_0_), channel_id=1, source_target_pairs={{2,0},{3,1},{0,2},{1,3},{6,4},{7,5},{4,6},{5,7},{10,8},{11,9},{8,1... | collective-permute-start | bytes 491528 | tf_op jit(solution)/shard_map/ppermute | solution.py:428
  175.4 7.6 %collective-permute-start.12 = (bf16[64,1280]{1,0:T(8,128)(2,1)S(1)}, bf16[64,1280]{1,0:T(8,128)(2,1)S(1)}, u32[]{:S(2)}, u32[]{:S(2)}) collective-permute-start(bf16[64,1280]{1,0:T(8,128)(2,1)S(1)} %get-tuple-element.21.refs_0_), channel_id=1, source_target_pairs={{1,0},{2,1},{3,2},{0,3},{5,4},{6,5},{7,6},{4,7},{9,8},{10,9},{11,1... | collective-permute-start | bytes 491528 | tf_op jit(solution)/shard_map/ppermute | solution.py:428
  176.4 6.2 %collective-permute-start.19 = (f32[1536]{0:T(1024)S(1)}, f32[1536]{0:T(1024)S(1)}, u32[]{:S(2)}, u32[]{:S(2)}) collective-permute-start(f32[1536]{0:T(1024)S(1)} %fusion.108), channel_id=1, source_target_pairs={{0,2},{1,3},{2,0},{3,1},{4,6},{5,7},{6,4},{7,5},{8,10},{9,11},{10,... | collective-permute-start | bytes 18440 | tf_op jit(solution)/shard_map/ppermute | solution.py:65
  187.7 106.2 %all-to-all-start.2 = ((bf16[64,8,4224]{2,1,0:T(8,128)(2,1)}), bf16[64,8,4224]{2,1,0:T(8,128)(2,1)}, u32[]{:S(2)}, u32[]{:S(2)}) async-start(bf16[64,8,4224]{2,1,0:T(8,128)(2,1)} %bitcast.28), calls=%async_computation.2 | async-start | bytes 8650752 | tf_op jit(solution)/shard_map/all_to_all | solution.py:18
  195.1 12.1 %collective-permute-start.11 = (bf16[64,256]{1,0:T(8,128)(2,1)S(1)}, bf16[64,256]{1,0:T(8,128)(2,1)S(1)}, u32[]{:S(2)}, u32[]{:S(2)}) collective-permute-start(bf16[64,256]{1,0:T(8,128)(2,1)S(1)} %get-tuple-element.29), channel_id=1, source_target_pairs={{3,0},{0,1},{1,2},{2,3},{7,4},{4,5},{5,6},{6,7},{11,8},{8,9},{9,10... | collective-permute-start | bytes 98312 | tf_op jit(solution)/shard_map/ppermute | solution.py:428
  196.5 10.7 %collective-permute-start.10 = (bf16[64,256]{1,0:T(8,128)(2,1)S(1)}, bf16[64,256]{1,0:T(8,128)(2,1)S(1)}, u32[]{:S(2)}, u32[]{:S(2)}) collective-permute-start(bf16[64,256]{1,0:T(8,128)(2,1)S(1)} %get-tuple-element.29), channel_id=1, source_target_pairs={{2,0},{3,1},{0,2},{1,3},{6,4},{7,5},{4,6},{5,7},{10,8},{11,9},{8,1... | collective-permute-start | bytes 98312 | tf_op jit(solution)/shard_map/ppermute | solution.py:428
  198.9 8.3 %collective-permute-start.9 = (bf16[64,256]{1,0:T(8,128)(2,1)S(1)}, bf16[64,256]{1,0:T(8,128)(2,1)S(1)}, u32[]{:S(2)}, u32[]{:S(2)}) collective-permute-start(bf16[64,256]{1,0:T(8,128)(2,1)S(1)} %get-tuple-element.29), channel_id=1, source_target_pairs={{1,0},{2,1},{3,2},{0,3},{5,4},{6,5},{7,6},{4,7},{9,8},{10,9},{11,1... | collective-permute-start | bytes 98312 | tf_op jit(solution)/shard_map/ppermute | solution.py:428
  203.8 3.5 %copy-start.5 = (bf16[256,1024]{1,0:T(8,128)(2,1)S(1)}, bf16[256,1024]{1,0:T(8,128)(2,1)}, u32[]{:S(2)}) copy-start(bf16[256,1024]{1,0:T(8,128)(2,1)} %param.8) | copy-start | bytes 1572868
  208.0 6.2 %collective-permute-start.17 = (f32[256]{0:T(256)S(1)}, f32[256]{0:T(256)S(1)}, u32[]{:S(2)}, u32[]{:S(2)}) collective-permute-start(f32[256]{0:T(256)S(1)} %fusion.15), channel_id=1, source_target_pairs={{0,3},{1,0},{2,1},{3,2},{4,7},{5,4},{6,5},{7,6},{8,11},{9,8},{10,9... | collective-permute-start | bytes 3080 | tf_op jit(solution)/shard_map/ppermute | solution.py:73
  208.6 5.6 %collective-permute-start.16 = (f32[256]{0:T(256)S(1)}, f32[256]{0:T(256)S(1)}, u32[]{:S(2)}, u32[]{:S(2)}) collective-permute-start(f32[256]{0:T(256)S(1)} %fusion.15), channel_id=1, source_target_pairs={{0,2},{1,3},{2,0},{3,1},{4,6},{5,7},{6,4},{7,5},{8,10},{9,11},{10,... | collective-permute-start | bytes 3080 | tf_op jit(solution)/shard_map/ppermute | solution.py:73
  211.1 4.0 %collective-permute-start.15 = (f32[256]{0:T(256)S(1)}, f32[256]{0:T(256)S(1)}, u32[]{:S(2)}, u32[]{:S(2)}) collective-permute-start(f32[256]{0:T(256)S(1)} %fusion.15), channel_id=1, source_target_pairs={{0,1},{1,2},{2,3},{3,0},{4,5},{5,6},{6,7},{7,4},{8,9},{9,10},{10,1... | collective-permute-start | bytes 3080 | tf_op jit(solution)/shard_map/ppermute | solution.py:73
  211.4 1.1 copy-start.7
  215.5 1.9 copy-start.9
  296.6 24.6 %all-to-all-start.3 = ((bf16[64,4,1152]{2,1,0:T(4,128)(2,1)}), bf16[64,4,1152]{2,1,0:T(4,128)(2,1)}, u32[]{:S(2)}, u32[]{:S(2)}) async-start(bf16[64,4,1152]{2,1,0:T(4,128)(2,1)} %all_to_all.30), calls=%async_computation.3 | async-start | bytes 1179648 | tf_op jit(solution)/shard_map/all_to_all | solution.py:18
  310.1 12.7 %copy-start.6 = (bf16[256,1024]{1,0:T(8,128)(2,1)S(1)}, bf16[256,1024]{1,0:T(8,128)(2,1)}, u32[]{:S(2)}) copy-start(bf16[256,1024]{1,0:T(8,128)(2,1)} %param.8) | copy-start | bytes 1572868
  310.1 12.7 %copy-start.8 = (f32[256,1024]{1,0:T(8,128)S(1)}, f32[256,1024]{1,0:T(8,128)}, u32[]{:S(2)}) copy-start(f32[256,1024]{1,0:T(8,128)} %copy-done.7) | copy-start | bytes 3145732

commit v3 on v2

--- a/solution.py
+++ b/solution.py
@@ -55,8 +55,7 @@
 
 
 def after(x, value):
-    corner = lax.slice(value, (0,) * value.ndim, (1,) * value.ndim).astype(F32)
-    return jnp.where(jnp.isnan(corner).reshape((1,) * x.ndim), jnp.zeros_like(x), x)
+    return jnp.where(jnp.isnan(value.reshape(-1)[0].astype(F32)), jnp.zeros_like(x), x)
 
 
 def folded(x):
@@ -118,48 +117,39 @@
     pool, features = emb_pool.shape
     lines = rows // chunk * GROUP
     halves = GROUP // chunk
-
-    def body(masks_ref, first_ref, pool_ref, out_ref, digits_ref):
-        step = pl.program_id(0)
-        line = sublanes_of((lines, 1))
+    tile = lines // 2
+
+    def body(masks_ref, first_ref, pool_ref, out_ref):
+        line = sublanes_of((tile, 1)) + pl.program_id(0) * tile
         receiver = line // GROUP
         part = (line % GROUP) // chunk
         piece = line % chunk
-
-        @pl.when(step == 0)
-        def _():
-            spreading = hot(lanes_of((lines, rows)) == receiver * chunk + piece)
-            digits_ref[...] = dot(spreading, first_ref[:, features:])
-
-        @pl.when(step < steps)
-        def _():
-            digits = digits_ref[...]
-            lane = lanes_of(digits.shape)
+        home = receiver * chunk + piece
+        digits = dot(hot(lanes_of((tile, rows)) == home), first_ref[:, features:])
+        lane = lanes_of(digits.shape)
+        for step in range(steps):
             place = step * halves + part
             value = jnp.where(lane == place, digits * 16.0, 0.0)
             value = jnp.where(lane == place + 64, digits, value)
             asked = jnp.sum(value, axis=1, keepdims=True).astype(jnp.int32) - 1
-            out_ref[...] = dot(hot(lanes_of((lines, pool)) == asked), pool_ref[...]).astype(BF)
-
-        @pl.when(step == steps)
-        def _():
-            mask = jnp.where(part == 0, masks_ref[0], masks_ref[1])
-            source = (receiver ^ mask) * chunk + piece
-            chosen = hot(lanes_of((lines, rows)) == source)
-            out_ref[...] = dot(chosen, first_ref[:, :features]).astype(BF)
-
+            out = dot(hot(lanes_of((tile, pool)) == asked), pool_ref[...]).astype(BF)
+            out_ref[:, step * features : (step + 1) * features] = out
+        mask = jnp.where(part == 0, masks_ref[0], masks_ref[1])
+        chosen = hot(lanes_of((tile, rows)) == (receiver ^ mask) * chunk + piece)
+        out_ref[:, steps * features :] = dot(chosen, first_ref[:, :features]).astype(BF)
+
+    width_out = (steps + 1) * features
     return called(
         body,
-        pltpu.HBM((lines, (steps + 1) * features), BF),
+        pltpu.HBM((lines, width_out), BF),
         2 * lines * steps * pool * features,
-        grid=(steps + 1,),
+        grid=(lines // tile,),
         in_specs=[
             pl.BlockSpec(memory_space=pltpu.SMEM),
             whole((rows, width)),
             whole((pool, features)),
         ],
-        out_specs=pl.BlockSpec((lines, features), lambda i: (0, i)),
-        scratch_shapes=[pltpu.VMEM((lines, 128), F32)],
+        out_specs=pl.BlockSpec((tile, width_out), lambda i: (i, 0)),
     )(masks, first, emb_pool)
 
 

time: 325 us -> 323 us (level)
  transfers between devices with their start and end apart: 24 -> 24, of which waited for: 10 -> 10; matrix products, arithmetic and copies ran while one was open for 7% -> 8% of each run, Pallas kernels for 4% -> 4%
where the time goes in v3:
time: 323 us; the launch traced here: 322 us
  waiting for transfers between devices  196 us (61%)
  starting transfers between devices  56.6 us (18%)
  Pallas kernels  23.1 us (7%)
  matrix products  11.4 us (4%)
  other arithmetic  11.3 us (3%)
  local copies, waits for them, and re-layouts  10.3 us (3%)
  blocking collectives  8.54 us (3%)
  between operations  5.13 us (2%)
    all_to_all x4, waiting for transfers between devices, exchanged(): return lax.all_to_all(x, 'batch', split_axis=0, concat_axis=0, tiled=True)  181 us
    all_to_all x4, starting transfers between devices, exchanged(): return lax.all_to_all(x, 'batch', split_axis=0, concat_axis=0, tiled=True)  33.1 us
    dot_general x10, matrix products, dot(): return lax.dot_general(a, b, (dims, ((), ())), preferred_element_type=F32)  11.4 us
    ppermute x3, waiting for transfers between devices, per_device(): lax.ppermute(coded[step - 1], 'mp', [(i, (i + step) % parts) for i in ran...  8.73 us
    psum x1, blocking collectives, per_device(): lax.psum(jnp.concatenate([row_squares(x, late_gain) for x in (query_hidde...  8.54 us
    ppermute x6, starting transfers between devices, gathered(): lax.ppermute(piece, 'mp', [((i + step) % parts, i) for i in range(parts)])  7.95 us
    ppermute x6, starting transfers between devices, summed(): lax.ppermute(x, 'mp', [(i, (i + step) % parts) for i in range(parts)])  7.73 us
  transfers between devices with their start and end apart: 24, of which 10 were waited for; matrix products, arithmetic and copies ran while one was open for 8% of the time, Pallas kernels for 4%

profile of v3, /device:TPU:1, one launch (start us, length us, event | category | flops | bytes accessed | tf_op | source)
XLA Modules:
  0.0 322.0 jit_solution(7660225599416557389)
XLA Ops:
  0.7 1.3 multiply_reduce_fusion
  2.0 3.6 %collective-permute-start.2 = (f32[256]{0:T(256)S(1)}, f32[256]{0:T(256)S(1)}, u32[]{:S(2)}, u32[]{:S(2)}) collective-permute-start(f32[256]{0:T(256)S(1)} %multiply_reduce_fusion), channel_id=1, source_target_pairs={{0,3},{1,0},{2,1},{3,2},{4,7},{5,4},{6,5},{7,6},{8,11},{9,8},{10,9... | collective-permute-start | bytes 3080 | tf_op jit(solution)/shard_map/ppermute | solution.py:72
  6.7 0.7 and_bitcast_fusion
  7.4 0.9 fusion.79
  9.2 0.9 convolution_convert_fusion
  10.7 1.1 pad_maximum_fusion
  11.8 13.4 %all-to-all-start = ((bf16[64,4,1152]{2,1,0:T(4,128)(2,1)}), bf16[64,4,1152]{2,1,0:T(4,128)(2,1)}, u32[]{:S(2)}, u32[]{:S(2)}) async-start(bf16[64,4,1152]{2,1,0:T(4,128)(2,1)} %pad_maximum_fusion), calls=%async_computation | async-start | bytes 1179648 | tf_op jit(solution)/shard_map/all_to_all | solution.py:18
  25.8 8.5 %psum.7 = f32[768]{0:T(1024)S(1)} all-reduce(f32[768]{0:T(1024)S(1)} %pad_maximum_fusion.5), channel_id=1, replica_groups=mesh['batch'=64,'mp'=4] {'mp'}, use_global_device_ids=true, to_apply=%region_5.6 | all-reduce | flops 768 | bytes 6144 | tf_op jit(solution)/shard_map/psum | solution.py:371
  34.6 9.2 %all-to-all-done = bf16[64,4,1152]{2,1,0:T(4,128)(2,1)} async-done(((bf16[64,4,1152]{2,1,0:T(4,128)(2,1)}), bf16[64,4,1152]{2,1,0:T(4,128)(2,1)}, u32[]{:S(2)}, u32[]{:S(2)}) %all-to-all-start) | async-done | bytes 589856 | tf_op jit(solution)/shard_map/all_to_all | solution.py:18
  43.8 1.5 reshape.422.first_ref
  45.3 4.8 %shard_map.102 = bf16[512,4096]{1,0:T(8,128)(2,1)} custom-call(s32[2]{0:T(128)S(1)} %copy-done.2, bf16[256,1152]{1,0:T(8,128)(2,1)S(1)} %reshape.422.first_ref, bf16[512,1024]{1,0:T(8,128)(2,1)S(1)} %fusion.7.pool_ref), custom_call_target="tpu_custom_call" | custom-call | flops 1610612736 | bytes 8388608 | tf_op jit(solution)/shard_map/pallas_call | solution.py:142
  50.1 6.5 %all-to-all-start.1 = ((bf16[64,8,4096]{2,1,0:T(8,128)(2,1)}), bf16[64,8,4096]{2,1,0:T(8,128)(2,1)}, u32[]{:S(2)}, u32[]{:S(2)}) async-start(bf16[64,8,4096]{2,1,0:T(8,128)(2,1)} %bitcast.34), calls=%async_computation.1 | async-start | bytes 8388608 | tf_op jit(solution)/shard_map/all_to_all | solution.py:18
  58.1 2.2 reshape_reshape.3
  60.3 1.2 slice.115
  62.8 1.5 fusion.75
  65.0 1.7 collective-permute-start.5
  66.7 1.4 collective-permute-start.4
  68.1 84.4 %all-to-all-done.1 = bf16[64,8,4096]{2,1,0:T(8,128)(2,1)} async-done(((bf16[64,8,4096]{2,1,0:T(8,128)(2,1)}), bf16[64,8,4096]{2,1,0:T(8,128)(2,1)}, u32[]{:S(2)}, u32[]{:S(2)}) %all-to-all-start.1) | async-done | bytes 4194336 | tf_op jit(solution)/shard_map/all_to_all | solution.py:18
  152.5 5.8 %shard_map.103 = (f32[64,1280]{1,0:T(8,128)S(1)}, s16[64,1280]{1,0:T(8,128)(2,1)S(1)}, s16[64,1280]{1,0:T(8,128)(2,1)S(1)}, s16[64,1280]{1,0:T(8,128)(2,1)S(1)}) custom-call(bf16[256,1024]{1,0:T(8,128)(2,1)S(1)} %fusion.38.q_ref.refs_7_, bf16[512,4096]{1,0:T(8,128)(2,1)} %bitcast.7.arrived_ref, s32[768,1]{1,0:T(8,128)S(1)} %fusion.47.code_ref), custom_call_target="tpu_custom_call" | custom-call | flops 2415919104 | bytes 8388608 | tf_op jit(solution)/shard_map/pallas_call | solution.py:189
  158.3 1.8 collective-permute-start.8
  160.1 1.4 collective-permute-start.7
  161.6 1.0 exponential_reduce_fusion.1
  162.5 1.3 collective-permute-done.8
  163.8 2.9 collective-permute-done.7
  166.8 4.5 %collective-permute-done.6 = s16[64,1280]{1,0:T(8,128)(2,1)S(1)} collective-permute-done((s16[64,1280]{1,0:T(8,128)(2,1)S(1)}, s16[64,1280]{1,0:T(8,128)(2,1)S(1)}, u32[]{:S(2)}, u32[]{:S(2)}) %collective-permute-start.6) | collective-permute-done | bytes 163872 | tf_op jit(solution)/shard_map/ppermute | solution.py:401
  172.0 1.5 collective-permute-start.14
  173.5 1.4 collective-permute-start.13
  174.9 1.0 collective-permute-start.12
  175.9 1.4 collective-permute-start.19
  177.3 4.8 %collective-permute-done.19 = f32[1536]{0:T(1024)S(1)} collective-permute-done((f32[1536]{0:T(1024)S(1)}, f32[1536]{0:T(1024)S(1)}, u32[]{:S(2)}, u32[]{:S(2)}) %collective-permute-start.19) | collective-permute-done | bytes 6176 | tf_op jit(solution)/shard_map/ppermute | solution.py:64
  182.4 4.7 %shard_map.104 = bf16[512,4224]{1,0:T(8,128)(2,1)} custom-call(bf16[64,1280]{1,0:T(8,128)(2,1)S(1)} %get-tuple-element.21.refs_0_, bf16[64,1280]{1,0:T(8,128)(2,1)S(1)} %collective-permute-done.12.refs_1_, bf16[64,1280]{1,0:T(8,128)(2,1)S(1)} %collective-permute-done.13.refs_2_, bf16[64,1280]{1,0:T(8,128)(2,1)S(1)} %collective-permute-done.14.refs_3_, ...), custom_call_target="tpu_custom_call" | custom-call | flops 1879048192 | bytes 8388608 | tf_op jit(solution)/shard_map/pallas_call | solution.py:238
  187.1 7.4 %all-to-all-start.2 = ((bf16[64,8,4224]{2,1,0:T(8,128)(2,1)}), bf16[64,8,4224]{2,1,0:T(8,128)(2,1)}, u32[]{:S(2)}, u32[]{:S(2)}) async-start(bf16[64,8,4224]{2,1,0:T(8,128)(2,1)} %bitcast.33), calls=%async_computation.2 | async-start | bytes 8650752 | tf_op jit(solution)/shard_map/all_to_all | solution.py:18
  194.6 1.4 collective-permute-start.11
  196.0 2.4 collective-permute-start.10
  198.7 1.1 fusion.1
  199.9 1.7 fusion.27
  201.6 1.7 fusion.29
  203.2 1.7 fusion.31
  205.0 1.7 fusion.25
  208.1 2.4 collective-permute-start.16
  210.8 1.1 copy-done.3
  216.9 76.4 %all-to-all-done.2 = bf16[64,8,4224]{2,1,0:T(8,128)(2,1)} async-done(((bf16[64,8,4224]{2,1,0:T(8,128)(2,1)}), bf16[64,8,4224]{2,1,0:T(8,128)(2,1)}, u32[]{:S(2)}, u32[]{:S(2)}) %all-to-all-start.2) | async-done | bytes 4325408 | tf_op jit(solution)/shard_map/all_to_all | solution.py:18
  293.3 1.8 shard_map.105
  295.1 1.0 all_to_all.30
  296.1 5.8 %all-to-all-start.3 = ((bf16[64,4,1152]{2,1,0:T(4,128)(2,1)}), bf16[64,4,1152]{2,1,0:T(4,128)(2,1)S(1)}, u32[]{:S(2)}, u32[]{:S(2)}) async-start(bf16[64,4,1152]{2,1,0:T(4,128)(2,1)} %all_to_all.30), calls=%async_computation.3 | async-start | bytes 1179648 | tf_op jit(solution)/shard_map/all_to_all | solution.py:18
  303.4 5.9 %shard_map.106 = bf16[512,1024]{1,0:T(8,128)(2,1)} custom-call(bf16[512,4224]{1,0:T(8,128)(2,1)} %bitcast.12.near_ref.extra_ref.third_ref, s32[3,512]{1,0:T(4,128)S(1)} %reshape.426.asked_ref, bf16[512,1024]{1,0:T(8,128)(2,1)S(1)} %copy-done, f32[512,1]{1,0:T(8,128)S(1)} %copy.34.inverse_ref, f32[1,1024]{1,0:T(1,128)S(1)} %bitcast.30), custom_call_target="tpu_custom_call" | custom-call | flops 1610612736 | bytes 8388608 | tf_op jit(solution)/shard_map/pallas_call | solution.py:308
  309.4 11.2 %all-to-all-done.3 = bf16[64,4,1152]{2,1,0:T(4,128)(2,1)S(1)} async-done(((bf16[64,4,1152]{2,1,0:T(4,128)(2,1)}), bf16[64,4,1152]{2,1,0:T(4,128)(2,1)S(1)}, u32[]{:S(2)}, u32[]{:S(2)}) %all-to-all-start.3) | async-done | bytes 589856 | tf_op jit(solution)/shard_map/all_to_all | solution.py:18
  320.8 1.1 fusion.24
  (105 shorter events, 12.7 us)
Async XLA Ops:
  0.6 9.6 %copy-start.6 = (bf16[256,1024]{1,0:T(8,128)(2,1)S(1)}, bf16[256,1024]{1,0:T(8,128)(2,1)}, u32[]{:S(2)}) copy-start(bf16[256,1024]{1,0:T(8,128)(2,1)} %param.8) | copy-start | bytes 1572868
  0.6 9.6 %copy-start.1 = (f32[1024]{0:T(1024)S(1)}, f32[1024]{0:T(1024)}, u32[]{:S(2)}) copy-start(f32[1024]{0:T(1024)} %param.10) | copy-start | bytes 12292
  2.0 8.2 %collective-permute-start.2 = (f32[256]{0:T(256)S(1)}, f32[256]{0:T(256)S(1)}, u32[]{:S(2)}, u32[]{:S(2)}) collective-permute-start(f32[256]{0:T(256)S(1)} %multiply_reduce_fusion), channel_id=1, source_target_pairs={{0,3},{1,0},{2,1},{3,2},{4,7},{5,4},{6,5},{7,6},{8,11},{9,8},{10,9... | collective-permute-start | bytes 3080 | tf_op jit(solution)/shard_map/ppermute | solution.py:72
  5.6 4.6 %collective-permute-start.1 = (f32[256]{0:T(256)S(1)}, f32[256]{0:T(256)S(1)}, u32[]{:S(2)}, u32[]{:S(2)}) collective-permute-start(f32[256]{0:T(256)S(1)} %multiply_reduce_fusion), channel_id=1, source_target_pairs={{0,2},{1,3},{2,0},{3,1},{4,6},{5,7},{6,4},{7,5},{8,10},{9,11},{10,... | collective-permute-start | bytes 3080 | tf_op jit(solution)/shard_map/ppermute | solution.py:72
  6.0 4.2 %collective-permute-start = (f32[256]{0:T(256)S(1)}, f32[256]{0:T(256)S(1)}, u32[]{:S(2)}, u32[]{:S(2)}) collective-permute-start(f32[256]{0:T(256)S(1)} %multiply_reduce_fusion), channel_id=1, source_target_pairs={{0,1},{1,2},{2,3},{3,0},{4,5},{5,6},{6,7},{7,4},{8,9},{9,10},{10,1... | collective-permute-start | bytes 3080 | tf_op jit(solution)/shard_map/ppermute | solution.py:72
  10.4 14.8 %copy-start.5 = (bf16[256,1024]{1,0:T(8,128)(2,1)S(1)}, bf16[256,1024]{1,0:T(8,128)(2,1)}, u32[]{:S(2)}) copy-start(bf16[256,1024]{1,0:T(8,128)(2,1)} %param.7) | copy-start | bytes 1572868
  10.4 15.0 %copy-start = (bf16[512,1024]{1,0:T(8,128)(2,1)S(1)}, bf16[512,1024]{1,0:T(8,128)(2,1)}, u32[]{:S(2)}) copy-start(bf16[512,1024]{1,0:T(8,128)(2,1)} %hidden_ref.1) | copy-start | bytes 3145732
  11.8 32.1 %all-to-all-start = ((bf16[64,4,1152]{2,1,0:T(4,128)(2,1)}), bf16[64,4,1152]{2,1,0:T(4,128)(2,1)}, u32[]{:S(2)}, u32[]{:S(2)}) async-start(bf16[64,4,1152]{2,1,0:T(4,128)(2,1)} %pad_maximum_fusion), calls=%async_computation | async-start | bytes 1179648 | tf_op jit(solution)/shard_map/all_to_all | solution.py:18
  25.4 19.9 %copy-start.2 = (s32[2]{0:T(128)S(1)}, s32[2]{0:T(128)}, u32[]{:S(2)}) copy-start(s32[2]{0:T(128)} %masks_ref.1) | copy-start | bytes 28
  50.1 102.4 %all-to-all-start.1 = ((bf16[64,8,4096]{2,1,0:T(8,128)(2,1)}), bf16[64,8,4096]{2,1,0:T(8,128)(2,1)}, u32[]{:S(2)}, u32[]{:S(2)}) async-start(bf16[64,8,4096]{2,1,0:T(8,128)(2,1)} %bitcast.34), calls=%async_computation.1 | async-start | bytes 8388608 | tf_op jit(solution)/shard_map/all_to_all | solution.py:18
  65.0 96.6 %collective-permute-start.5 = (f32[64,256]{1,0:T(8,128)}, f32[64,256]{1,0:T(8,128)S(1)}, u32[]{:S(2)}, u32[]{:S(2)}) collective-permute-start(f32[64,256]{1,0:T(8,128)} %get-tuple-element.23), channel_id=1, source_target_pairs={{0,3},{1,0},{2,1},{3,2},{4,7},{5,4},{6,5},{7,6},{8,11},{9,8},{10,9... | collective-permute-start | bytes 196616 | tf_op jit(solution)/shard_map/ppermute | solution.py:392
  66.7 94.8 %collective-permute-start.4 = (f32[64,256]{1,0:T(8,128)}, f32[64,256]{1,0:T(8,128)S(1)}, u32[]{:S(2)}, u32[]{:S(2)}) collective-permute-start(f32[64,256]{1,0:T(8,128)} %get-tuple-element.24), channel_id=1, source_target_pairs={{0,2},{1,3},{2,0},{3,1},{4,6},{5,7},{6,4},{7,5},{8,10},{9,11},{10,... | collective-permute-start | bytes 196616 | tf_op jit(solution)/shard_map/ppermute | solution.py:392
  68.1 93.4 %collective-permute-start.3 = (f32[64,256]{1,0:T(8,128)}, f32[64,256]{1,0:T(8,128)}, u32[]{:S(2)}, u32[]{:S(2)}) collective-permute-start(f32[64,256]{1,0:T(8,128)} %get-tuple-element.22), channel_id=1, source_target_pairs={{0,1},{1,2},{2,3},{3,0},{4,5},{5,6},{6,7},{7,4},{8,9},{9,10},{10,1... | collective-permute-start | bytes 196616 | tf_op jit(solution)/shard_map/ppermute | solution.py:392
  158.3 5.5 %collective-permute-start.8 = (s16[64,1280]{1,0:T(8,128)(2,1)S(1)}, s16[64,1280]{1,0:T(8,128)(2,1)S(1)}, u32[]{:S(2)}, u32[]{:S(2)}) collective-permute-start(s16[64,1280]{1,0:T(8,128)(2,1)S(1)} %get-tuple-element.11), channel_id=1, source_target_pairs={{0,3},{1,0},{2,1},{3,2},{4,7},{5,4},{6,5},{7,6},{8,11},{9,8},{10,9... | collective-permute-start | bytes 491528 | tf_op jit(solution)/shard_map/ppermute | solution.py:401
  160.1 6.6 %collective-permute-start.7 = (s16[64,1280]{1,0:T(8,128)(2,1)S(1)}, s16[64,1280]{1,0:T(8,128)(2,1)S(1)}, u32[]{:S(2)}, u32[]{:S(2)}) collective-permute-start(s16[64,1280]{1,0:T(8,128)(2,1)S(1)} %get-tuple-element.10), channel_id=1, source_target_pairs={{0,2},{1,3},{2,0},{3,1},{4,6},{5,7},{6,4},{7,5},{8,10},{9,11},{10,... | collective-permute-start | bytes 491528 | tf_op jit(solution)/shard_map/ppermute | solution.py:401
  161.5 9.7 %collective-permute-start.6 = (s16[64,1280]{1,0:T(8,128)(2,1)S(1)}, s16[64,1280]{1,0:T(8,128)(2,1)S(1)}, u32[]{:S(2)}, u32[]{:S(2)}) collective-permute-start(s16[64,1280]{1,0:T(8,128)(2,1)S(1)} %get-tuple-element.9), channel_id=1, source_target_pairs={{0,1},{1,2},{2,3},{3,0},{4,5},{5,6},{6,7},{7,4},{8,9},{9,10},{10,1... | collective-permute-start | bytes 491528 | tf_op jit(solution)/shard_map/ppermute | solution.py:401
  171.9 4.0 %collective-permute-start.18 = (f32[1536]{0:T(1024)S(1)}, f32[1536]{0:T(1024)S(1)}, u32[]{:S(2)}, u32[]{:S(2)}) collective-permute-start(f32[1536]{0:T(1024)S(1)} %maximum_multiply_fusion), channel_id=1, source_target_pairs={{0,1},{1,0},{2,3},{3,2},{4,5},{5,4},{6,7},{7,6},{8,9},{9,8},{10,11... | collective-permute-start | bytes 18440 | tf_op jit(solution)/shard_map/ppermute | solution.py:64
  172.0 10.1 %collective-permute-start.14 = (bf16[64,1280]{1,0:T(8,128)(2,1)S(1)}, bf16[64,1280]{1,0:T(8,128)(2,1)S(1)}, u32[]{:S(2)}, u32[]{:S(2)}) collective-permute-start(bf16[64,1280]{1,0:T(8,128)(2,1)S(1)} %get-tuple-element.21.refs_0_), channel_id=1, source_target_pairs={{3,0},{0,1},{1,2},{2,3},{7,4},{4,5},{5,6},{6,7},{11,8},{8,9},{9,10... | collective-permute-start | bytes 491528 | tf_op jit(solution)/shard_map/ppermute | solution.py:418
  173.5 8.6 %collective-permute-start.13 = (bf16[64,1280]{1,0:T(8,128)(2,1)S(1)}, bf16[64,1280]{1,0:T(8,128)(2,1)S(1)}, u32[]{:S(2)}, u32[]{:S(2)}) collective-permute-start(bf16[64,1280]{1,0:T(8,128)(2,1)S(1)} %get-tuple-element.21.refs_0_), channel_id=1, source_target_pairs={{2,0},{3,1},{0,2},{1,3},{6,4},{7,5},{4,6},{5,7},{10,8},{11,9},{8,1... | collective-permute-start | bytes 491528 | tf_op jit(solution)/shard_map/ppermute | solution.py:418
  174.9 7.6 %collective-permute-start.12 = (bf16[64,1280]{1,0:T(8,128)(2,1)S(1)}, bf16[64,1280]{1,0:T(8,128)(2,1)S(1)}, u32[]{:S(2)}, u32[]{:S(2)}) collective-permute-start(bf16[64,1280]{1,0:T(8,128)(2,1)S(1)} %get-tuple-element.21.refs_0_), channel_id=1, source_target_pairs={{1,0},{2,1},{3,2},{0,3},{5,4},{6,5},{7,6},{4,7},{9,8},{10,9},{11,1... | collective-permute-start | bytes 491528 | tf_op jit(solution)/shard_map/ppermute | solution.py:418
  175.9 6.2 %collective-permute-start.19 = (f32[1536]{0:T(1024)S(1)}, f32[1536]{0:T(1024)S(1)}, u32[]{:S(2)}, u32[]{:S(2)}) collective-permute-start(f32[1536]{0:T(1024)S(1)} %fusion.108), channel_id=1, source_target_pairs={{0,2},{1,3},{2,0},{3,1},{4,6},{5,7},{6,4},{7,5},{8,10},{9,11},{10,... | collective-permute-start | bytes 18440 | tf_op jit(solution)/shard_map/ppermute | solution.py:64
  187.1 106.2 %all-to-all-start.2 = ((bf16[64,8,4224]{2,1,0:T(8,128)(2,1)}), bf16[64,8,4224]{2,1,0:T(8,128)(2,1)}, u32[]{:S(2)}, u32[]{:S(2)}) async-start(bf16[64,8,4224]{2,1,0:T(8,128)(2,1)} %bitcast.33), calls=%async_computation.2 | async-start | bytes 8650752 | tf_op jit(solution)/shard_map/all_to_all | solution.py:18
  194.6 12.1 %collective-permute-start.11 = (bf16[64,256]{1,0:T(8,128)(2,1)S(1)}, bf16[64,256]{1,0:T(8,128)(2,1)S(1)}, u32[]{:S(2)}, u32[]{:S(2)}) collective-permute-start(bf16[64,256]{1,0:T(8,128)(2,1)S(1)} %get-tuple-element.29), channel_id=1, source_target_pairs={{3,0},{0,1},{1,2},{2,3},{7,4},{4,5},{5,6},{6,7},{11,8},{8,9},{9,10... | collective-permute-start | bytes 98312 | tf_op jit(solution)/shard_map/ppermute | solution.py:418
  196.0 10.7 %collective-permute-start.10 = (bf16[64,256]{1,0:T(8,128)(2,1)S(1)}, bf16[64,256]{1,0:T(8,128)(2,1)S(1)}, u32[]{:S(2)}, u32[]{:S(2)}) collective-permute-start(bf16[64,256]{1,0:T(8,128)(2,1)S(1)} %get-tuple-element.29), channel_id=1, source_target_pairs={{2,0},{3,1},{0,2},{1,3},{6,4},{7,5},{4,6},{5,7},{10,8},{11,9},{8,1... | collective-permute-start | bytes 98312 | tf_op jit(solution)/shard_map/ppermute | solution.py:418
  198.4 8.3 %collective-permute-start.9 = (bf16[64,256]{1,0:T(8,128)(2,1)S(1)}, bf16[64,256]{1,0:T(8,128)(2,1)S(1)}, u32[]{:S(2)}, u32[]{:S(2)}) collective-permute-start(bf16[64,256]{1,0:T(8,128)(2,1)S(1)} %get-tuple-element.29), channel_id=1, source_target_pairs={{1,0},{2,1},{3,2},{0,3},{5,4},{6,5},{7,6},{4,7},{9,8},{10,9},{11,1... | collective-permute-start | bytes 98312 | tf_op jit(solution)/shard_map/ppermute | solution.py:418
  203.2 3.5 %copy-start.7 = (bf16[256,1024]{1,0:T(8,128)(2,1)S(1)}, bf16[256,1024]{1,0:T(8,128)(2,1)}, u32[]{:S(2)}) copy-start(bf16[256,1024]{1,0:T(8,128)(2,1)} %param.8) | copy-start | bytes 1572868
  207.5 6.4 %collective-permute-start.17 = (f32[256]{0:T(256)S(1)}, f32[256]{0:T(256)S(1)}, u32[]{:S(2)}, u32[]{:S(2)}) collective-permute-start(f32[256]{0:T(256)S(1)} %fusion.15), channel_id=1, source_target_pairs={{0,3},{1,0},{2,1},{3,2},{4,7},{5,4},{6,5},{7,6},{8,11},{9,8},{10,9... | collective-permute-start | bytes 3080 | tf_op jit(solution)/shard_map/ppermute | solution.py:72
  208.1 5.9 %collective-permute-start.16 = (f32[256]{0:T(256)S(1)}, f32[256]{0:T(256)S(1)}, u32[]{:S(2)}, u32[]{:S(2)}) collective-permute-start(f32[256]{0:T(256)S(1)} %fusion.15), channel_id=1, source_target_pairs={{0,2},{1,3},{2,0},{3,1},{4,6},{5,7},{6,4},{7,5},{8,10},{9,11},{10,... | collective-permute-start | bytes 3080 | tf_op jit(solution)/shard_map/ppermute | solution.py:72
  210.5 4.0 %collective-permute-start.15 = (f32[256]{0:T(256)S(1)}, f32[256]{0:T(256)S(1)}, u32[]{:S(2)}, u32[]{:S(2)}) collective-permute-start(f32[256]{0:T(256)S(1)} %fusion.15), channel_id=1, source_target_pairs={{0,1},{1,2},{2,3},{3,0},{4,5},{5,6},{6,7},{7,4},{8,9},{9,10},{10,1... | collective-permute-start | bytes 3080 | tf_op jit(solution)/shard_map/ppermute | solution.py:72
  210.8 1.1 copy-start.3
  214.9 2.0 copy-start.9
  296.1 24.5 %all-to-all-start.3 = ((bf16[64,4,1152]{2,1,0:T(4,128)(2,1)}), bf16[64,4,1152]{2,1,0:T(4,128)(2,1)S(1)}, u32[]{:S(2)}, u32[]{:S(2)}) async-start(bf16[64,4,1152]{2,1,0:T(4,128)(2,1)} %all_to_all.30), calls=%async_computation.3 | async-start | bytes 1179648 | tf_op jit(solution)/shard_map/all_to_all | solution.py:18
  309.4 11.4 %copy-start.4 = (f32[256,1024]{1,0:T(8,128)S(1)}, f32[256,1024]{1,0:T(8,128)}, u32[]{:S(2)}) copy-start(f32[256,1024]{1,0:T(8,128)} %copy-done.3) | copy-start | bytes 3145732
  309.4 11.5 %copy-start.8 = (bf16[256,1024]{1,0:T(8,128)(2,1)S(1)}, bf16[256,1024]{1,0:T(8,128)(2,1)}, u32[]{:S(2)}) copy-start(bf16[256,1024]{1,0:T(8,128)(2,1)} %param.8) | copy-start | bytes 1572868

commit v4 on v3

--- a/solution.py
+++ b/solution.py
@@ -397,7 +397,8 @@
     scores_own = scores_own / SOFTMAX_TEMPER
     kept, *coded = partial_scores(turned_q, arrived, code, steps, parts)
     total = jnp.zeros_like(kept)
-    for step in range(1, parts):
+    by_distance = sorted(range(1, parts), key=lambda step: min(step, parts - step))
+    for step in by_distance:
         total = total + lax.ppermute(
             coded[step - 1], "mp", [(i, (i + step) % parts) for i in range(parts)]
         ).astype(F32)
@@ -412,12 +413,12 @@
     weights_far = (exp_far * ratio[:, None] * SCALE).astype(BF)
 
     def gathered(piece):
-        pieces = [piece]
-        for step in range(1, parts):
-            pieces.append(
-                lax.ppermute(piece, "mp", [((i + step) % parts, i) for i in range(parts)])
+        pieces = {0: piece}
+        for step in by_distance:
+            pieces[step] = lax.ppermute(
+                piece, "mp", [((i + step) % parts, i) for i in range(parts)]
             )
-        return pieces
+        return [pieces[step] for step in range(parts)]
 
     far_pieces = gathered(weights_far)
     values = folded(

time: 323 us -> 322 us (level)
  waiting for transfers between devices: 196 us -> 192 us
  transfers between devices with their start and end apart: 24 -> 24, of which waited for: 10 -> 9; matrix products, arithmetic and copies ran while one was open for 8% -> 8% of each run, Pallas kernels for 4% -> 4%
where the time goes in v4:
time: 322 us; the launch traced here: 321 us
  waiting for transfers between devices  192 us (60%)
  starting transfers between devices  59 us (18%)
  Pallas kernels  23.1 us (7%)
  matrix products  11.4 us (4%)
  other arithmetic  11.3 us (4%)
  local copies, waits for them, and re-layouts  10.3 us (3%)
  blocking collectives  8.54 us (3%)
  between operations  5.13 us (2%)
    all_to_all x4, waiting for transfers between devices, exchanged(): return lax.all_to_all(x, 'batch', split_axis=0, concat_axis=0, tiled=True)  181 us
    all_to_all x4, starting transfers between devices, exchanged(): return lax.all_to_all(x, 'batch', split_axis=0, concat_axis=0, tiled=True)  34.2 us
    dot_general x10, matrix products, dot(): return lax.dot_general(a, b, (dims, ((), ())), preferred_element_type=F32)  11.4 us
    ppermute x6, starting transfers between devices, gathered(): lax.ppermute(piece, 'mp', [((i + step) % parts, i) for i in range(parts)])  9.06 us
    psum x1, blocking collectives, per_device(): lax.psum(jnp.concatenate([row_squares(x, late_gain) for x in (query_hidde...  8.54 us
    ppermute x6, starting transfers between devices, summed(): lax.ppermute(x, 'mp', [(i, (i + step) % parts) for i in range(parts)])  7.51 us
  transfers between devices with their start and end apart: 24, of which 9 were waited for; matrix products, arithmetic and copies ran while one was open for 8% of the time, Pallas kernels for 4%

profile of v4, /device:TPU:1, one launch (start us, length us, event | category | flops | bytes accessed | tf_op | source)
XLA Modules:
  0.0 320.9 jit_solution(18187725979453542882)
XLA Ops:
  0.7 1.3 multiply_reduce_fusion
  2.0 3.6 %collective-permute-start.2 = (f32[256]{0:T(256)S(1)}, f32[256]{0:T(256)S(1)}, u32[]{:S(2)}, u32[]{:S(2)}) collective-permute-start(f32[256]{0:T(256)S(1)} %multiply_reduce_fusion), channel_id=1, source_target_pairs={{0,3},{1,0},{2,1},{3,2},{4,7},{5,4},{6,5},{7,6},{8,11},{9,8},{10,9... | collective-permute-start | bytes 3080 | tf_op jit(solution)/shard_map/ppermute | solution.py:72
  6.0 0.7 collective-permute-start
  6.7 0.7 and_bitcast_fusion
  7.4 0.9 fusion.79
  9.2 0.9 convolution_convert_fusion
  10.7 1.1 pad_maximum_fusion
  11.8 13.4 %all-to-all-start = ((bf16[64,4,1152]{2,1,0:T(4,128)(2,1)}), bf16[64,4,1152]{2,1,0:T(4,128)(2,1)}, u32[]{:S(2)}, u32[]{:S(2)}) async-start(bf16[64,4,1152]{2,1,0:T(4,128)(2,1)} %pad_maximum_fusion), calls=%async_computation | async-start | bytes 1179648 | tf_op jit(solution)/shard_map/all_to_all | solution.py:18
  25.8 8.5 %psum.7 = f32[768]{0:T(1024)S(1)} all-reduce(f32[768]{0:T(1024)S(1)} %pad_maximum_fusion.5), channel_id=1, replica_groups=mesh['batch'=64,'mp'=4] {'mp'}, use_global_device_ids=true, to_apply=%region_5.6 | all-reduce | flops 768 | bytes 6144 | tf_op jit(solution)/shard_map/psum | solution.py:371
  34.6 9.2 %all-to-all-done = bf16[64,4,1152]{2,1,0:T(4,128)(2,1)} async-done(((bf16[64,4,1152]{2,1,0:T(4,128)(2,1)}), bf16[64,4,1152]{2,1,0:T(4,128)(2,1)}, u32[]{:S(2)}, u32[]{:S(2)}) %all-to-all-start) | async-done | bytes 589856 | tf_op jit(solution)/shard_map/all_to_all | solution.py:18
  43.8 1.5 reshape.422.first_ref
  45.3 4.8 %shard_map.102 = bf16[512,4096]{1,0:T(8,128)(2,1)} custom-call(s32[2]{0:T(128)S(1)} %copy-done.2, bf16[256,1152]{1,0:T(8,128)(2,1)S(1)} %reshape.422.first_ref, bf16[512,1024]{1,0:T(8,128)(2,1)S(1)} %fusion.7.pool_ref), custom_call_target="tpu_custom_call" | custom-call | flops 1610612736 | bytes 8388608 | tf_op jit(solution)/shard_map/pallas_call | solution.py:142
  50.1 6.5 %all-to-all-start.1 = ((bf16[64,8,4096]{2,1,0:T(8,128)(2,1)}), bf16[64,8,4096]{2,1,0:T(8,128)(2,1)}, u32[]{:S(2)}, u32[]{:S(2)}) async-start(bf16[64,8,4096]{2,1,0:T(8,128)(2,1)} %bitcast.34), calls=%async_computation.1 | async-start | bytes 8388608 | tf_op jit(solution)/shard_map/all_to_all | solution.py:18
  58.1 2.2 reshape_reshape.3
  60.3 1.2 slice.115
  62.8 1.5 fusion.75
  65.0 1.7 collective-permute-start.5
  66.7 1.4 collective-permute-start.4
  68.1 84.4 %all-to-all-done.1 = bf16[64,8,4096]{2,1,0:T(8,128)(2,1)} async-done(((bf16[64,8,4096]{2,1,0:T(8,128)(2,1)}), bf16[64,8,4096]{2,1,0:T(8,128)(2,1)}, u32[]{:S(2)}, u32[]{:S(2)}) %all-to-all-start.1) | async-done | bytes 4194336 | tf_op jit(solution)/shard_map/all_to_all | solution.py:18
  152.5 5.8 %shard_map.103 = (f32[64,1280]{1,0:T(8,128)S(1)}, s16[64,1280]{1,0:T(8,128)(2,1)S(1)}, s16[64,1280]{1,0:T(8,128)(2,1)S(1)}, s16[64,1280]{1,0:T(8,128)(2,1)S(1)}) custom-call(bf16[256,1024]{1,0:T(8,128)(2,1)S(1)} %fusion.38.q_ref.refs_7_, bf16[512,4096]{1,0:T(8,128)(2,1)} %bitcast.7.arrived_ref, s32[768,1]{1,0:T(8,128)S(1)} %fusion.47.code_ref), custom_call_target="tpu_custom_call" | custom-call | flops 2415919104 | bytes 8388608 | tf_op jit(solution)/shard_map/pallas_call | solution.py:189
  158.3 1.5 collective-permute-start.8
  159.8 2.3 collective-permute-start.7
  162.2 1.0 exponential_reduce_fusion.1
  163.1 2.2 collective-permute-done.8
  165.3 2.9 collective-permute-done.7
  168.2 0.8 collective-permute-done.6
  169.6 0.9 collective-permute-start.18
  171.2 2.1 collective-permute-start.13
  173.3 2.0 collective-permute-start.12
  175.7 4.4 %collective-permute-done.19 = f32[1536]{0:T(1024)S(1)} collective-permute-done((f32[1536]{0:T(1024)S(1)}, f32[1536]{0:T(1024)S(1)}, u32[]{:S(2)}, u32[]{:S(2)}) %collective-permute-start.19) | collective-permute-done | bytes 6176 | tf_op jit(solution)/shard_map/ppermute | solution.py:64
  180.2 4.7 %shard_map.104 = bf16[512,4224]{1,0:T(8,128)(2,1)} custom-call(bf16[64,1280]{1,0:T(8,128)(2,1)S(1)} %get-tuple-element.21.refs_0_, bf16[64,1280]{1,0:T(8,128)(2,1)S(1)} %collective-permute-done.12.refs_1_, bf16[64,1280]{1,0:T(8,128)(2,1)S(1)} %collective-permute-done.13.refs_2_, bf16[64,1280]{1,0:T(8,128)(2,1)S(1)} %collective-permute-done.14.refs_3_, ...), custom_call_target="tpu_custom_call" | custom-call | flops 1879048192 | bytes 8388608 | tf_op jit(solution)/shard_map/pallas_call | solution.py:238
  184.9 8.6 %all-to-all-start.2 = ((bf16[64,8,4224]{2,1,0:T(8,128)(2,1)}), bf16[64,8,4224]{2,1,0:T(8,128)(2,1)}, u32[]{:S(2)}, u32[]{:S(2)}) async-start(bf16[64,8,4224]{2,1,0:T(8,128)(2,1)} %bitcast.33), calls=%async_computation.2 | async-start | bytes 8650752 | tf_op jit(solution)/shard_map/all_to_all | solution.py:18
  193.5 1.6 collective-permute-start.11
  195.1 2.2 collective-permute-start.10
  197.9 1.1 fusion.1
  199.0 1.7 fusion.27
  200.7 1.7 fusion.29
  202.4 1.7 fusion.31
  204.1 1.7 fusion.25
  207.2 2.2 collective-permute-start.16
  209.8 1.1 copy-done.3
  215.9 76.4 %all-to-all-done.2 = bf16[64,8,4224]{2,1,0:T(8,128)(2,1)} async-done(((bf16[64,8,4224]{2,1,0:T(8,128)(2,1)}), bf16[64,8,4224]{2,1,0:T(8,128)(2,1)}, u32[]{:S(2)}, u32[]{:S(2)}) %all-to-all-start.2) | async-done | bytes 4325408 | tf_op jit(solution)/shard_map/all_to_all | solution.py:18
  292.2 1.8 shard_map.105
  294.1 1.0 all_to_all.30
  295.0 5.8 %all-to-all-start.3 = ((bf16[64,4,1152]{2,1,0:T(4,128)(2,1)}), bf16[64,4,1152]{2,1,0:T(4,128)(2,1)S(1)}, u32[]{:S(2)}, u32[]{:S(2)}) async-start(bf16[64,4,1152]{2,1,0:T(4,128)(2,1)} %all_to_all.30), calls=%async_computation.3 | async-start | bytes 1179648 | tf_op jit(solution)/shard_map/all_to_all | solution.py:18
  302.4 5.9 %shard_map.106 = bf16[512,1024]{1,0:T(8,128)(2,1)} custom-call(bf16[512,4224]{1,0:T(8,128)(2,1)} %bitcast.12.near_ref.extra_ref.third_ref, s32[3,512]{1,0:T(4,128)S(1)} %reshape.426.asked_ref, bf16[512,1024]{1,0:T(8,128)(2,1)S(1)} %copy-done, f32[512,1]{1,0:T(8,128)S(1)} %copy.34.inverse_ref, f32[1,1024]{1,0:T(1,128)S(1)} %bitcast.30), custom_call_target="tpu_custom_call" | custom-call | flops 1610612736 | bytes 8388608 | tf_op jit(solution)/shard_map/pallas_call | solution.py:308
  308.3 11.2 %all-to-all-done.3 = bf16[64,4,1152]{2,1,0:T(4,128)(2,1)S(1)} async-done(((bf16[64,4,1152]{2,1,0:T(4,128)(2,1)}), bf16[64,4,1152]{2,1,0:T(4,128)(2,1)S(1)}, u32[]{:S(2)}, u32[]{:S(2)}) %all-to-all-start.3) | async-done | bytes 589856 | tf_op jit(solution)/shard_map/all_to_all | solution.py:18
  319.8 1.1 fusion.24
  (105 shorter events, 12.8 us)
Async XLA Ops:
  0.6 9.6 %copy-start.6 = (bf16[256,1024]{1,0:T(8,128)(2,1)S(1)}, bf16[256,1024]{1,0:T(8,128)(2,1)}, u32[]{:S(2)}) copy-start(bf16[256,1024]{1,0:T(8,128)(2,1)} %param.8) | copy-start | bytes 1572868
  0.6 9.6 %copy-start.1 = (f32[1024]{0:T(1024)S(1)}, f32[1024]{0:T(1024)}, u32[]{:S(2)}) copy-start(f32[1024]{0:T(1024)} %param.10) | copy-start | bytes 12292
  2.0 8.2 %collective-permute-start.2 = (f32[256]{0:T(256)S(1)}, f32[256]{0:T(256)S(1)}, u32[]{:S(2)}, u32[]{:S(2)}) collective-permute-start(f32[256]{0:T(256)S(1)} %multiply_reduce_fusion), channel_id=1, source_target_pairs={{0,3},{1,0},{2,1},{3,2},{4,7},{5,4},{6,5},{7,6},{8,11},{9,8},{10,9... | collective-permute-start | bytes 3080 | tf_op jit(solution)/shard_map/ppermute | solution.py:72
  5.6 4.6 %collective-permute-start.1 = (f32[256]{0:T(256)S(1)}, f32[256]{0:T(256)S(1)}, u32[]{:S(2)}, u32[]{:S(2)}) collective-permute-start(f32[256]{0:T(256)S(1)} %multiply_reduce_fusion), channel_id=1, source_target_pairs={{0,2},{1,3},{2,0},{3,1},{4,6},{5,7},{6,4},{7,5},{8,10},{9,11},{10,... | collective-permute-start | bytes 3080 | tf_op jit(solution)/shard_map/ppermute | solution.py:72
  6.0 4.2 %collective-permute-start = (f32[256]{0:T(256)S(1)}, f32[256]{0:T(256)S(1)}, u32[]{:S(2)}, u32[]{:S(2)}) collective-permute-start(f32[256]{0:T(256)S(1)} %multiply_reduce_fusion), channel_id=1, source_target_pairs={{0,1},{1,2},{2,3},{3,0},{4,5},{5,6},{6,7},{7,4},{8,9},{9,10},{10,1... | collective-permute-start | bytes 3080 | tf_op jit(solution)/shard_map/ppermute | solution.py:72
  10.4 14.8 %copy-start.5 = (bf16[256,1024]{1,0:T(8,128)(2,1)S(1)}, bf16[256,1024]{1,0:T(8,128)(2,1)}, u32[]{:S(2)}) copy-start(bf16[256,1024]{1,0:T(8,128)(2,1)} %param.7) | copy-start | bytes 1572868
  10.4 15.0 %copy-start = (bf16[512,1024]{1,0:T(8,128)(2,1)S(1)}, bf16[512,1024]{1,0:T(8,128)(2,1)}, u32[]{:S(2)}) copy-start(bf16[512,1024]{1,0:T(8,128)(2,1)} %hidden_ref.1) | copy-start | bytes 3145732
  11.8 32.1 %all-to-all-start = ((bf16[64,4,1152]{2,1,0:T(4,128)(2,1)}), bf16[64,4,1152]{2,1,0:T(4,128)(2,1)}, u32[]{:S(2)}, u32[]{:S(2)}) async-start(bf16[64,4,1152]{2,1,0:T(4,128)(2,1)} %pad_maximum_fusion), calls=%async_computation | async-start | bytes 1179648 | tf_op jit(solution)/shard_map/all_to_all | solution.py:18
  25.4 19.9 %copy-start.2 = (s32[2]{0:T(128)S(1)}, s32[2]{0:T(128)}, u32[]{:S(2)}) copy-start(s32[2]{0:T(128)} %masks_ref.1) | copy-start | bytes 28
  50.1 102.4 %all-to-all-start.1 = ((bf16[64,8,4096]{2,1,0:T(8,128)(2,1)}), bf16[64,8,4096]{2,1,0:T(8,128)(2,1)}, u32[]{:S(2)}, u32[]{:S(2)}) async-start(bf16[64,8,4096]{2,1,0:T(8,128)(2,1)} %bitcast.34), calls=%async_computation.1 | async-start | bytes 8388608 | tf_op jit(solution)/shard_map/all_to_all | solution.py:18
  65.0 97.2 %collective-permute-start.5 = (f32[64,256]{1,0:T(8,128)}, f32[64,256]{1,0:T(8,128)S(1)}, u32[]{:S(2)}, u32[]{:S(2)}) collective-permute-start(f32[64,256]{1,0:T(8,128)} %get-tuple-element.23), channel_id=1, source_target_pairs={{0,3},{1,0},{2,1},{3,2},{4,7},{5,4},{6,5},{7,6},{8,11},{9,8},{10,9... | collective-permute-start | bytes 196616 | tf_op jit(solution)/shard_map/ppermute | solution.py:392
  66.7 95.5 %collective-permute-start.4 = (f32[64,256]{1,0:T(8,128)}, f32[64,256]{1,0:T(8,128)S(1)}, u32[]{:S(2)}, u32[]{:S(2)}) collective-permute-start(f32[64,256]{1,0:T(8,128)} %get-tuple-element.24), channel_id=1, source_target_pairs={{0,2},{1,3},{2,0},{3,1},{4,6},{5,7},{6,4},{7,5},{8,10},{9,11},{10,... | collective-permute-start | bytes 196616 | tf_op jit(solution)/shard_map/ppermute | solution.py:392
  68.1 94.1 %collective-permute-start.3 = (f32[64,256]{1,0:T(8,128)}, f32[64,256]{1,0:T(8,128)}, u32[]{:S(2)}, u32[]{:S(2)}) collective-permute-start(f32[64,256]{1,0:T(8,128)} %get-tuple-element.22), channel_id=1, source_target_pairs={{0,1},{1,2},{2,3},{3,0},{4,5},{5,6},{6,7},{7,4},{8,9},{9,10},{10,1... | collective-permute-start | bytes 196616 | tf_op jit(solution)/shard_map/ppermute | solution.py:392
  158.3 7.0 %collective-permute-start.8 = (s16[64,1280]{1,0:T(8,128)(2,1)S(1)}, s16[64,1280]{1,0:T(8,128)(2,1)S(1)}, u32[]{:S(2)}, u32[]{:S(2)}) collective-permute-start(s16[64,1280]{1,0:T(8,128)(2,1)S(1)} %get-tuple-element.11), channel_id=1, source_target_pairs={{0,2},{1,3},{2,0},{3,1},{4,6},{5,7},{6,4},{7,5},{8,10},{9,11},{10,... | collective-permute-start | bytes 491528 | tf_op jit(solution)/shard_map/ppermute | solution.py:402
  159.8 8.4 %collective-permute-start.7 = (s16[64,1280]{1,0:T(8,128)(2,1)S(1)}, s16[64,1280]{1,0:T(8,128)(2,1)S(1)}, u32[]{:S(2)}, u32[]{:S(2)}) collective-permute-start(s16[64,1280]{1,0:T(8,128)(2,1)S(1)} %get-tuple-element.10), channel_id=1, source_target_pairs={{0,3},{1,0},{2,1},{3,2},{4,7},{5,4},{6,5},{7,6},{8,11},{9,8},{10,9... | collective-permute-start | bytes 491528 | tf_op jit(solution)/shard_map/ppermute | solution.py:402
  162.1 6.8 %collective-permute-start.6 = (s16[64,1280]{1,0:T(8,128)(2,1)S(1)}, s16[64,1280]{1,0:T(8,128)(2,1)S(1)}, u32[]{:S(2)}, u32[]{:S(2)}) collective-permute-start(s16[64,1280]{1,0:T(8,128)(2,1)S(1)} %get-tuple-element.9), channel_id=1, source_target_pairs={{0,1},{1,2},{2,3},{3,0},{4,5},{5,6},{6,7},{7,4},{8,9},{9,10},{10,1... | collective-permute-start | bytes 491528 | tf_op jit(solution)/shard_map/ppermute | solution.py:402
  169.6 5.6 %collective-permute-start.18 = (f32[1536]{0:T(1024)S(1)}, f32[1536]{0:T(1024)S(1)}, u32[]{:S(2)}, u32[]{:S(2)}) collective-permute-start(f32[1536]{0:T(1024)S(1)} %maximum_multiply_fusion), channel_id=1, source_target_pairs={{0,1},{1,0},{2,3},{3,2},{4,5},{5,4},{6,7},{7,6},{8,9},{9,8},{10,11... | collective-permute-start | bytes 18440 | tf_op jit(solution)/shard_map/ppermute | solution.py:64
  170.5 9.6 %collective-permute-start.14 = (bf16[64,1280]{1,0:T(8,128)(2,1)S(1)}, bf16[64,1280]{1,0:T(8,128)(2,1)S(1)}, u32[]{:S(2)}, u32[]{:S(2)}) collective-permute-start(bf16[64,1280]{1,0:T(8,128)(2,1)S(1)} %get-tuple-element.21.refs_0_), channel_id=1, source_target_pairs={{3,0},{0,1},{1,2},{2,3},{7,4},{4,5},{5,6},{6,7},{11,8},{8,9},{9,10... | collective-permute-start | bytes 491528 | tf_op jit(solution)/shard_map/ppermute | solution.py:418
  171.2 9.0 %collective-permute-start.13 = (bf16[64,1280]{1,0:T(8,128)(2,1)S(1)}, bf16[64,1280]{1,0:T(8,128)(2,1)S(1)}, u32[]{:S(2)}, u32[]{:S(2)}) collective-permute-start(bf16[64,1280]{1,0:T(8,128)(2,1)S(1)} %get-tuple-element.21.refs_0_), channel_id=1, source_target_pairs={{2,0},{3,1},{0,2},{1,3},{6,4},{7,5},{4,6},{5,7},{10,8},{11,9},{8,1... | collective-permute-start | bytes 491528 | tf_op jit(solution)/shard_map/ppermute | solution.py:418
  173.3 6.9 %collective-permute-start.12 = (bf16[64,1280]{1,0:T(8,128)(2,1)S(1)}, bf16[64,1280]{1,0:T(8,128)(2,1)S(1)}, u32[]{:S(2)}, u32[]{:S(2)}) collective-permute-start(bf16[64,1280]{1,0:T(8,128)(2,1)S(1)} %get-tuple-element.21.refs_0_), channel_id=1, source_target_pairs={{1,0},{2,1},{3,2},{0,3},{5,4},{6,5},{7,6},{4,7},{9,8},{10,9},{11,1... | collective-permute-start | bytes 491528 | tf_op jit(solution)/shard_map/ppermute | solution.py:418
  175.3 4.9 %collective-permute-start.19 = (f32[1536]{0:T(1024)S(1)}, f32[1536]{0:T(1024)S(1)}, u32[]{:S(2)}, u32[]{:S(2)}) collective-permute-start(f32[1536]{0:T(1024)S(1)} %fusion.108), channel_id=1, source_target_pairs={{0,2},{1,3},{2,0},{3,1},{4,6},{5,7},{6,4},{7,5},{8,10},{9,11},{10,... | collective-permute-start | bytes 18440 | tf_op jit(solution)/shard_map/ppermute | solution.py:64
  184.9 107.3 %all-to-all-start.2 = ((bf16[64,8,4224]{2,1,0:T(8,128)(2,1)}), bf16[64,8,4224]{2,1,0:T(8,128)(2,1)}, u32[]{:S(2)}, u32[]{:S(2)}) async-start(bf16[64,8,4224]{2,1,0:T(8,128)(2,1)} %bitcast.33), calls=%async_computation.2 | async-start | bytes 8650752 | tf_op jit(solution)/shard_map/all_to_all | solution.py:18
  193.5 12.3 %collective-permute-start.11 = (bf16[64,256]{1,0:T(8,128)(2,1)S(1)}, bf16[64,256]{1,0:T(8,128)(2,1)S(1)}, u32[]{:S(2)}, u32[]{:S(2)}) collective-permute-start(bf16[64,256]{1,0:T(8,128)(2,1)S(1)} %get-tuple-element.29), channel_id=1, source_target_pairs={{3,0},{0,1},{1,2},{2,3},{7,4},{4,5},{5,6},{6,7},{11,8},{8,9},{9,10... | collective-permute-start | bytes 98312 | tf_op jit(solution)/shard_map/ppermute | solution.py:418
  195.1 10.7 %collective-permute-start.10 = (bf16[64,256]{1,0:T(8,128)(2,1)S(1)}, bf16[64,256]{1,0:T(8,128)(2,1)S(1)}, u32[]{:S(2)}, u32[]{:S(2)}) collective-permute-start(bf16[64,256]{1,0:T(8,128)(2,1)S(1)} %get-tuple-element.29), channel_id=1, source_target_pairs={{2,0},{3,1},{0,2},{1,3},{6,4},{7,5},{4,6},{5,7},{10,8},{11,9},{8,1... | collective-permute-start | bytes 98312 | tf_op jit(solution)/shard_map/ppermute | solution.py:418
  197.3 8.5 %collective-permute-start.9 = (bf16[64,256]{1,0:T(8,128)(2,1)S(1)}, bf16[64,256]{1,0:T(8,128)(2,1)S(1)}, u32[]{:S(2)}, u32[]{:S(2)}) collective-permute-start(bf16[64,256]{1,0:T(8,128)(2,1)S(1)} %get-tuple-element.29), channel_id=1, source_target_pairs={{1,0},{2,1},{3,2},{0,3},{5,4},{6,5},{7,6},{4,7},{9,8},{10,9},{11,1... | collective-permute-start | bytes 98312 | tf_op jit(solution)/shard_map/ppermute | solution.py:418
  202.4 3.5 %copy-start.7 = (bf16[256,1024]{1,0:T(8,128)(2,1)S(1)}, bf16[256,1024]{1,0:T(8,128)(2,1)}, u32[]{:S(2)}) copy-start(bf16[256,1024]{1,0:T(8,128)(2,1)} %param.8) | copy-start | bytes 1572868
  206.6 6.2 %collective-permute-start.17 = (f32[256]{0:T(256)S(1)}, f32[256]{0:T(256)S(1)}, u32[]{:S(2)}, u32[]{:S(2)}) collective-permute-start(f32[256]{0:T(256)S(1)} %fusion.15), channel_id=1, source_target_pairs={{0,3},{1,0},{2,1},{3,2},{4,7},{5,4},{6,5},{7,6},{8,11},{9,8},{10,9... | collective-permute-start | bytes 3080 | tf_op jit(solution)/shard_map/ppermute | solution.py:72
  207.2 5.6 %collective-permute-start.16 = (f32[256]{0:T(256)S(1)}, f32[256]{0:T(256)S(1)}, u32[]{:S(2)}, u32[]{:S(2)}) collective-permute-start(f32[256]{0:T(256)S(1)} %fusion.15), channel_id=1, source_target_pairs={{0,2},{1,3},{2,0},{3,1},{4,6},{5,7},{6,4},{7,5},{8,10},{9,11},{10,... | collective-permute-start | bytes 3080 | tf_op jit(solution)/shard_map/ppermute | solution.py:72
  209.4 4.0 %collective-permute-start.15 = (f32[256]{0:T(256)S(1)}, f32[256]{0:T(256)S(1)}, u32[]{:S(2)}, u32[]{:S(2)}) collective-permute-start(f32[256]{0:T(256)S(1)} %fusion.15), channel_id=1, source_target_pairs={{0,1},{1,2},{2,3},{3,0},{4,5},{5,6},{6,7},{7,4},{8,9},{9,10},{10,1... | collective-permute-start | bytes 3080 | tf_op jit(solution)/shard_map/ppermute | solution.py:72
  209.7 1.1 copy-start.3
  213.8 2.0 copy-start.9
  295.0 24.5 %all-to-all-start.3 = ((bf16[64,4,1152]{2,1,0:T(4,128)(2,1)}), bf16[64,4,1152]{2,1,0:T(4,128)(2,1)S(1)}, u32[]{:S(2)}, u32[]{:S(2)}) async-start(bf16[64,4,1152]{2,1,0:T(4,128)(2,1)} %all_to_all.30), calls=%async_computation.3 | async-start | bytes 1179648 | tf_op jit(solution)/shard_map/all_to_all | solution.py:18
  308.3 11.4 %copy-start.4 = (f32[256,1024]{1,0:T(8,128)S(1)}, f32[256,1024]{1,0:T(8,128)}, u32[]{:S(2)}) copy-start(f32[256,1024]{1,0:T(8,128)} %copy-done.3) | copy-start | bytes 3145732
  308.3 11.5 %copy-start.8 = (bf16[256,1024]{1,0:T(8,128)(2,1)S(1)}, bf16[256,1024]{1,0:T(8,128)(2,1)}, u32[]{:S(2)}) copy-start(bf16[256,1024]{1,0:T(8,128)(2,1)} %param.8) | copy-start | bytes 1572868
